TPU v7x, 256 devices: a whole 4x4x8 slice. The times are simulated.
256 devices in a mesh: prow: 16 (over z, y_hi), pcol: 16 (over x, y_lo, core).
Axes of the slice: x: 4, y: 4 (y_hi: 2, y_lo: 2; y = y_hi * 2 + y_lo), z: 8, core: 2. Of those that a mesh axis runs over, the one named last changes fastest.
Arguments:
- root_inv: float32 [4096, 4096], P('prow', 'pcol'), may hold values from -2 to 2, as said below
- child_inv: float32 [4096, 4096], P('prow', 'pcol'), may hold values from -2 to 2, as said below
- child_panel: float32 [2048, 4096], P('prow', 'pcol'), may hold values from -0.25 to 0.25
- structure: int32 [16], replicated, may hold values from 0 to 31, as said below
Outputs:
- root_cov: float32 [4096, 4096], P('prow', 'pcol')
- cross_cov: float32 [4096, 4096], P('prow', 'pcol')
- child_cov: float32 [4096, 4096], P('prow', 'pcol')
Inputs may be any that keep to these rules, and one draw needn't show every extreme that they name: `root_inv`: lower triangular with a positive diagonal. `child_inv`: lower triangular with a positive diagonal. `structure`: 16 distinct root block numbers in increasing order; the first is 0 and the last is 31.
All inputs are finite; a program needn't handle non-finite values.
Results may differ from a plain program's by a relative error of at most 0.00008.
Values sent between devices are 32-bit elements; how exact they have to be, the bound alone decides.
A program may use at most 64 MiB of HBM per device.

v0:
```python
import jax
import jax.numpy as jnp
from jax import lax
from jax.sharding import PartitionSpec as P

B = 128
RBLK = 32
F = 16


def product(subscripts, former, latter):
    return jnp.einsum(
        subscripts,
        former,
        latter,
        precision=lax.Precision.HIGHEST,
        preferred_element_type=jnp.float32,
    )


def shards(root_inv, child_inv, child_panel, structure):
    row_count = root_inv.shape[0]
    col_count = child_inv.shape[1]
    row_base = lax.axis_index("prow") * row_count
    gathered_rows = lax.all_gather(child_panel, "prow", axis=0, tiled=True)
    selector = (jnp.arange(RBLK, dtype=jnp.int32)[:, None] == structure[None, :]).astype(
        jnp.float32
    )
    expanded = product("kf,fbq->kbq", selector, gathered_rows.reshape(F, B, col_count)).reshape(
        RBLK * B, col_count
    )
    row_block = (row_base + jnp.arange(row_count, dtype=jnp.int32)) // B
    row_live = jnp.sum((row_block[:, None] == structure[None, :]).astype(jnp.float32), axis=1)
    own_rows = lax.dynamic_slice_in_dim(expanded, row_base, row_count, 0)
    root_terms = product(
        "kr,kq->rq", lax.all_gather(root_inv, "pcol", axis=1, tiled=True), root_inv
    )
    root_cov = lax.psum_scatter(root_terms, "prow", scatter_dimension=0, tiled=True)
    initial = jnp.zeros((row_count, col_count), jnp.float32)
    cross = initial - product(
        "rk,kq->rq", lax.all_gather(root_cov, "pcol", axis=1, tiled=True), expanded
    )
    cross_cov = cross * row_live[:, None]
    inverse_terms = product(
        "kr,kq->rq", lax.all_gather(child_inv, "pcol", axis=1, tiled=True), child_inv
    )
    diag_cov = lax.psum_scatter(inverse_terms, "prow", scatter_dimension=0, tiled=True)
    update_terms = product(
        "kr,kq->rq", lax.all_gather(cross_cov, "pcol", axis=1, tiled=True), own_rows
    )
    update = lax.psum_scatter(update_terms, "prow", scatter_dimension=0, tiled=True)
    child_cov = diag_cov - update
    return (root_cov, cross_cov, child_cov)


def solution(mesh):
    placed = (P("prow", "pcol"), P("prow", "pcol"), P("prow", "pcol"), P())
    return jax.shard_map(
        shards,
        mesh=mesh,
        in_specs=placed,
        out_specs=(P("prow", "pcol"), P("prow", "pcol"), P("prow", "pcol")),
        check_vma=False,
    )
```

profile of v0, /device:TPU:1, one launch (start us, length us, event | category | flops | bytes accessed | tf_op | source)
XLA Modules:
  0.0 921.5 jit_solution(13511836139768057230)
XLA Ops:
  7.2 0.7 all-gather.6.cloned.1.call-update
  7.9 0.0 reduce-scatter.4.cloned.1.call-start
  7.9 45.9 %all-gather.6.cloned.1.call-done = f32[256,4096]{1,0:T(8,128)} async-done(((f32[256,256]{1,0:T(8,128)}), f32[256,4096]{1,0:T(8,128)}) %all-gather.6.cloned.1.call-update) | async-done | bytes 4194320 | tf_op jit(solution)/shard_map/all_gather | solution.py:36
  53.9 10.8 %fusion.9 = f32[4096,256]{1,0:T(8,128)} fusion(f32[256,4096]{1,0:T(8,128)} %all-gather.6.cloned.1.call-done, f32[256,256]{1,0:T(8,128)} %param.4), kind=kOutput, calls=%fused_computation.15 | convolution fusion | flops 3221225472 | bytes 8650752 | tf_op jit(solution)/shard_map/kr,kq->rq/dot_general | solution.py:12
  64.8 0.0 all-gather.10.cloned.1.call-start
  64.8 0.7 all-gather.10.cloned.1.call-update
  65.6 206.7 %reduce-scatter.4.cloned.1.call-done = f32[256,256]{1,0:T(8,128)} async-done(((f32[4096,256]{1,0:T(8,128)}), f32[256,256]{1,0:T(8,128)}) %reduce-scatter.4.cloned.1.call-update) | async-done | bytes 262160 | tf_op jit(solution)/shard_map/reduce_scatter | solution.py:38
  272.3 0.5 all-gather.12.cloned.1.call-update
  272.9 0.2 all-gather.14.cloned.1.call-start
  273.1 0.1 convert_reduce_fusion
  273.2 86.5 %all-gather.10.cloned.1.call-done = f32[2048,256]{1,0:T(8,128)} async-done(((f32[128,256]{1,0:T(8,128)}), f32[2048,256]{1,0:T(8,128)}) %all-gather.10.cloned.1.call-update) | async-done | bytes 2097168 | tf_op jit(solution)/shard_map/all_gather | solution.py:25
  359.7 4.4 fusion
  364.1 4.4 copy.10
  368.5 34.1 %all-gather.8.cloned.1.call-done = f32[256,4096]{1,0:T(8,128)} async-done(((f32[256,256]{1,0:T(8,128)}), f32[256,4096]{1,0:T(8,128)}) %all-gather.8.cloned.1.call-update) | async-done | bytes 4194320 | tf_op jit(solution)/shard_map/all_gather | solution.py:41
  402.6 7.8 fusion.2
  410.4 0.3 reduce-scatter.6.cloned.1.call-start
  410.7 33.7 %all-gather.12.cloned.1.call-done = f32[256,4096]{1,0:T(8,128)} async-done(((f32[256,256]{1,0:T(8,128)}), f32[256,4096]{1,0:T(8,128)}) %all-gather.12.cloned.1.call-update) | async-done | bytes 4194320 | tf_op jit(solution)/shard_map/all_gather | solution.py:45
  444.4 10.8 %fusion.10 = f32[4096,256]{1,0:T(8,128)} fusion(f32[256,4096]{1,0:T(8,128)} %all-gather.12.cloned.1.call-done, f32[256,256]{1,0:T(8,128)S(1)} %copy-done), kind=kOutput, calls=%fused_computation.16 | convolution fusion | flops 3221225472 | bytes 8650752 | tf_op jit(solution)/shard_map/kr,kq->rq/dot_general | solution.py:12
  455.3 0.3 reduce-scatter.8.cloned.1.call-start
  455.6 31.2 %all-gather.14.cloned.1.call-done = f32[256,4096]{1,0:T(8,128)} async-done(((f32[256,256]{1,0:T(8,128)}), f32[256,4096]{1,0:T(8,128)}) %all-gather.14.cloned.1.call-update) | async-done | bytes 4194320 | tf_op jit(solution)/shard_map/all_gather | solution.py:49
  486.8 10.9 %fusion.3 = f32[4096,256]{1,0:T(8,128)} fusion(f32[256,4096]{1,0:T(8,128)} %all-gather.14.cloned.1.call-done, f32[4096,256]{1,0:T(8,128)} %bitcast.13, s32[]{:T(128)S(6)} %select_n.13), kind=kOutput, calls=%fused_computation.4 | convolution fusion | flops 3221225472 | bytes 8650756 | tf_op jit(solution)/shard_map/kr,kq->rq/dot_general | solution.py:12
  497.7 200.9 %reduce-scatter.6.cloned.1.call-done = f32[256,256]{1,0:T(8,128)} async-done(((f32[4096,256]{1,0:T(8,128)}), f32[256,256]{1,0:T(8,128)}) %reduce-scatter.6.cloned.1.call-update) | async-done | bytes 262160 | tf_op jit(solution)/shard_map/reduce_scatter | solution.py:47
  698.6 214.2 %reduce-scatter.8.cloned.1.call-done = f32[256,256]{1,0:T(8,128)} async-done(((f32[4096,256]{1,0:T(8,128)}), f32[256,256]{1,0:T(8,128)}) %reduce-scatter.8.cloned.1.call-update) | async-done | bytes 262160 | tf_op jit(solution)/shard_map/reduce_scatter | solution.py:51
  912.9 1.8 sub.14
  (13 shorter events, 0.2 us)
Async XLA Ops:
  7.2 46.7 %all-gather.6.cloned.1.call-start = ((), (), s32[]{:S(2)}) async-start(), calls=%async_computation.3 | async-start | bytes 4456448 | tf_op jit(solution)/shard_map/all_gather | solution.py:36
  7.9 264.4 %reduce-scatter.4.cloned.1.call-start = ((), (), s32[]{:S(2)}) async-start(), calls=%async_computation.4 | async-start | bytes 4456448 | tf_op jit(solution)/shard_map/reduce_scatter | solution.py:38
  64.7 208.4 %copy-start.1 = (s32[16]{0:T(128)S(1)}, s32[16]{0:T(128)}, u32[]{:S(2)}) copy-start(s32[16]{0:T(128)} %param.7) | copy-start | bytes 196
  64.8 294.9 %all-gather.10.cloned.1.call-start = ((), (), s32[]{:S(2)}) async-start(), calls=%async_computation.6 | async-start | bytes 2228224 | tf_op jit(solution)/shard_map/all_gather | solution.py:25
  65.5 337.1 %all-gather.8.cloned.1.call-start = ((), (), s32[]{:S(2)}) async-start(), calls=%async_computation.5 | async-start | bytes 4456448 | tf_op jit(solution)/shard_map/all_gather | solution.py:41
  272.3 172.1 %all-gather.12.cloned.1.call-start = ((), (), s32[]{:S(2)}) async-start(), calls=%async_computation.7 | async-start | bytes 4456448 | tf_op jit(solution)/shard_map/all_gather | solution.py:45
  272.9 213.9 %all-gather.14.cloned.1.call-start = ((), (), s32[]{:S(2)}) async-start(), calls=%async_computation.9 | async-start | bytes 4456448 | tf_op jit(solution)/shard_map/all_gather | solution.py:49
  402.6 41.8 %copy-start = (f32[256,256]{1,0:T(8,128)S(1)}, f32[256,256]{1,0:T(8,128)}, u32[]{:S(2)}) copy-start(f32[256,256]{1,0:T(8,128)} %param.5) | copy-start | bytes 786436
  410.4 288.2 %reduce-scatter.6.cloned.1.call-start = ((), (), s32[]{:S(2)}) async-start(), calls=%async_computation.8 | async-start | bytes 4456448 | tf_op jit(solution)/shard_map/reduce_scatter | solution.py:47
  455.3 457.6 %reduce-scatter.8.cloned.1.call-start = ((), (), s32[]{:S(2)}) async-start(), calls=%async_computation.10 | async-start | bytes 4456448 | tf_op jit(solution)/shard_map/reduce_scatter | solution.py:51
Sparse Core Ops, SparseCore 0:
  9.8 44.0 all-gather.5
  64.9 207.3 reduce-scatter.3
  275.2 84.4 all-gather.9
  362.0 40.5 all-gather.7
  404.4 39.9 all-gather.11
  446.8 39.9 all-gather.13
  491.3 207.2 reduce-scatter.5
  702.7 210.1 reduce-scatter.7
where the time goes:
time: 925 us; the launch traced here: 921 us
  waiting for transfers between devices  855 us (92%)
  matrix products  44.8 us (5%)
  between operations  14.2 us (2%)
    reduce_scatter x1, waiting for transfers between devices, shards(): lax.psum_scatter(update_terms, 'prow', scatter_dimension=0, tiled=True)  214 us
    reduce_scatter x1, waiting for transfers between devices, shards(): lax.psum_scatter(root_terms, 'prow', scatter_dimension=0, tiled=True)  207 us
    reduce_scatter x1, waiting for transfers between devices, shards(): lax.psum_scatter(inverse_terms, 'prow', scatter_dimension=0, tiled=True)  201 us
    all_gather x1, waiting for transfers between devices, shards(): gathered_rows = lax.all_gather(child_panel, 'prow', axis=0, tiled=True)  86.5 us
    all_gather x1, waiting for transfers between devices, shards(): lax.all_gather(root_inv, 'pcol', axis=1, tiled=True)  45.9 us
    dot_general x5, matrix products, product(): jnp.einsum(subscripts, former, latter, precision=lax.Precision.HIGHEST, p...  44.8 us
    all_gather x1, waiting for transfers between devices, shards(): lax.all_gather(root_cov, 'pcol', axis=1, tiled=True)  34.1 us
    all_gather x1, waiting for transfers between devices, shards(): lax.all_gather(child_inv, 'pcol', axis=1, tiled=True)  33.7 us
  transfers between devices with their start and end apart: 8, of which 8 were waited for; matrix products, arithmetic and copies ran while one was open for 4% of the time, Pallas kernels for 0%

commit v1 on v0

v1 whole, which is shorter than its diff:
```python
import jax
import jax.numpy as jnp
from jax import lax
from jax.experimental import pallas as pl
from jax.experimental.pallas import tpu as pltpu
from jax.sharding import PartitionSpec as P

MESH = pl.DeviceIdType.MESH
F32 = jnp.float32
BF16 = jnp.bfloat16
F = 16
N = 256
H = 128
Z = 8
R4 = 4


def split(v):
    hi = v.astype(BF16)
    return hi, (v - hi.astype(F32)).astype(BF16)


def dot3(a_hi, a_lo, b):
    b_hi, b_lo = split(b)
    out = jnp.dot(a_hi, b_hi, preferred_element_type=F32)
    out += jnp.dot(a_hi, b_lo, preferred_element_type=F32)
    return out + jnp.dot(a_lo, b_hi, preferred_element_type=F32)


def arrived(ref, sem):
    pltpu.make_async_copy(ref, ref, sem).wait()


class Sends:
    def __init__(self, sem):
        self.sem, self.count, self.open = sem, 0, []

    def go(self, src, dst, recv, dev, kind, when=None):
        pltpu.make_async_remote_copy(
            src_ref=src, dst_ref=dst, send_sem=self.sem.at[self.count], recv_sem=recv, device_id=dev, device_id_type=MESH
        ).start()
        self.open.append((self.count, kind, when))
        self.count += 1

    def drain(self):
        for when in dict.fromkeys(w for _, _, w in self.open):
            def body(when=when):
                for n, kind, w in self.open:
                    if w is when:
                        arrived(kind, self.sem.at[n])
            if when is None:
                body()
            else:
                pl.when(when.cond)(body)


class Cond:
    def __init__(self, cond):
        self.cond = cond


class Ring4:
    def __init__(self, sends, whole, half, pos, plus, minus, sems, kind, kind_half, lane, sib=None, when=None):
        self.__dict__.update(locals())
        self.near = (lax.rem(pos + 3, R4), lax.rem(pos + 1, R4))
        self.far = lax.rem(pos + 2, R4)

    def push(self, at, dev, which):
        self.sends.go(self.whole(at), self.whole(at), self.sems.at[self.lane, which], dev, self.kind, self.when)

    def start(self):
        self.push(self.pos, self.plus, 0)
        self.push(self.pos, self.minus, 1)
        if self.sib:
            self.sib(self.pos)

    def mid(self, side):
        at = self.near[side]
        arrived(self.whole(at), self.sems.at[self.lane, side])
        ref = self.half(at, side)
        dev = self.plus if side == 0 else self.minus
        self.sends.go(ref, ref, self.sems.at[self.lane, 2 + side], dev, self.kind_half, self.when)
        if self.sib:
            self.sib(at)

    def end(self):
        arrived(self.half(self.far, 0), self.sems.at[self.lane, 2])
        arrived(self.half(self.far, 1), self.sems.at[self.lane, 3])
        if self.sib:
            self.sib(self.far)


def kernel(
    st, r, l, p, root, cross, child,
    rg, lg, yg, lj, yj, rc, pg, rjt, ljt, yjt, troot, tchild, rsr, rsc,
    s_send, s_r1, s_r2, s_rsib, s_lj, s_ly, s_lx, s_lsib, s_yy, s_yx, s_ysib, s_cy, s_cx, s_csib, s_p, s_pw, s_zr, s_zc,
):
    row, col = lax.axis_index("prow"), lax.axis_index("pcol")
    z, yh = lax.div(row, 2), lax.rem(row, 2)
    x, yl, core = lax.div(col, 4), lax.rem(lax.div(col, 2), 2), lax.rem(col, 2)
    y = 2 * yh + yl

    def dev(zz, yy, xx, cc):
        return (2 * zz + lax.div(yy, 2), 4 * xx + 2 * lax.rem(yy, 2) + cc)

    def up(v, by, n):
        return lax.rem(v + by, n)

    xp, xm = dev(z, y, up(x, 1, 4), core), dev(z, y, up(x, 3, 4), core)
    yp, ym = dev(z, up(y, 1, 4), x, core), dev(z, up(y, 3, 4), x, core)
    zp, zm = dev(up(z, 1, Z), y, x, core), dev(up(z, 7, Z), y, x, core)
    sib = dev(z, y, x, 1 - core)
    yo = dev(z, up(y, 2, 4), x, core)
    pair = dev(z, 2 * yh + 1 - yl, x, core)
    cross_y = dev(z, 2 * (1 - yh) + 1 - yl, x, core)

    inside = Cond(core == yh)
    outside = Cond(core != yh)
    sends = Sends(s_send)

    rg[yh, pl.ds(2 * col, 1)] = r[:, 0:H].reshape(1, N, H)
    rg[yh, pl.ds(2 * col + 1, 1)] = r[:, H:N].reshape(1, N, H)
    pg[pl.ds(row, 1)] = p[...].reshape(1, H, N)
    lj[pl.ds(yh, 1)] = l[...].reshape(1, N, N)

    @pl.when(inside.cond)
    def _():
        lg[yh, pl.ds(lax.div(col, 2), 1)] = l[...].reshape(1, N, N)

    barrier = pltpu.get_barrier_semaphore()
    for d in (xp, xm, yp, ym, zp, zm, sib, yo):
        pl.semaphore_signal(barrier, inc=1, device_id=d, device_id_type=MESH)
    pl.semaphore_wait(barrier, 8)

    k_r, k_rh = rg.at[0, pl.ds(0, 2)], rg.at[0, 0]
    k_l, k_lh = lg.at[0, 0], lg.at[0, 0, pl.ds(0, H)]
    k_c, k_ch = rc.at[pl.ds(0, 2)], rc.at[0]

    a, b = x + core * (y - x), y + core * (x - y)

    def r_at(al, be):
        xx, yy = al + core * (be - al), be + core * (al - be)
        return lax.div(yy, 2), 4 * xx + 2 * lax.rem(yy, 2) + core, yy * 4 + xx

    def r_dev(al, be):
        return dev(z, be + core * (al - be), al + core * (be - al), core)

    def r_whole(al, be):
        u, q, _ = r_at(al, be)
        return rg.at[u, pl.ds(2 * q, 2)]

    def r_half(al, be, h):
        u, q, _ = r_at(al, be)
        return rg.at[u, 2 * q + h]

    def r_sib(al, be):
        u, q, n = r_at(al, be)
        ref = rg.at[u, pl.ds(2 * q, 2)]
        sends.go(ref, ref, s_rsib.at[n], sib, k_r)

    first = Ring4(
        sends, lambda at: r_whole(at, b), lambda at, h: r_half(at, b, h), a,
        r_dev(up(a, 1, 4), b), r_dev(up(a, 3, 4), b), s_r1, k_r, k_rh, 0,
    )
    second = []
    for k, off in enumerate((0, 3, 1, 2)):
        al = up(a, off, 4)
        second.append(Ring4(
            sends, lambda at, al=al: r_whole(al, at), lambda at, h, al=al: r_half(al, at, h), b,
            r_dev(a, up(b, 1, 4)), r_dev(a, up(b, 3, 4)), s_r2, k_r, k_rh, k,
            sib=lambda at, al=al: r_sib(al, at),
        ))

    def p_slot(lane, zz):
        return 2 * zz + (yh if lane == 0 else 1 - yh)

    def p_push(lane, zz, step, side):
        whole = step < 3
        n = p_slot(lane, zz)
        if whole:
            ref, kind = pg.at[n], pg.at[0]
        else:
            ref, kind = pg.at[n, pl.ds(64 * side, 64)], pg.at[0, pl.ds(0, 64)]
        sends.go(ref, ref, s_p.at[lane, side, step], zp if side == 0 else zm, kind)

    def p_start(lane):
        p_push(lane, z, 0, 0)
        p_push(lane, z, 0, 1)

    def p_step(lane, step):
        for side in range(2):
            zz = up(z, Z - step, Z) if side == 0 else up(z, step, Z)
            arrived(pg.at[p_slot(lane, zz)], s_p.at[lane, side, step - 1])
            p_push(lane, zz, step, side)

    def p_end(lane):
        n = p_slot(lane, up(z, 4, Z))
        for side in range(2):
            arrived(pg.at[n, pl.ds(64 * side, 64)], s_p.at[lane, side, 3])

    def l_sib(u, v):
        ref = lg.at[u, v]
        sends.go(ref, ref, s_lsib.at[u, v], sib, k_l, inside)

    def ring_x(buf, sems, sibling, lane, u, yy):
        return Ring4(
            sends, lambda at: buf.at[u, 2 * at + yy], lambda at, h: buf.at[u, 2 * at + yy, pl.ds(H * h, H)], x,
            xp, xm, sems, k_l, k_lh, lane, sib=lambda at: sibling(u, 2 * at + yy), when=inside,
        )

    l_lanes = [
        ring_x(lg, s_lx, l_sib, 0, yh, yl),
        ring_x(lg, s_lx, l_sib, 1, yh, 1 - yl),
        ring_x(lg, s_lx, l_sib, 2, 1 - yh, 1 - yl),
        ring_x(lg, s_lx, l_sib, 3, 1 - yh, yl),
    ]
    own_v = 2 * x + yl

    def l_y_start():
        @pl.when(inside.cond)
        def _():
            sends.go(lg.at[yh, own_v], lg.at[yh, own_v], s_ly.at[0], pair, k_l, inside)
            sends.go(lg.at[yh, own_v], lj.at[yh], s_lj.at[0], yo, k_l, inside)

        @pl.when(outside.cond)
        def _():
            sends.go(l, lg.at[yh, own_v], s_ly.at[1], cross_y, k_l, outside)

    def l_x_start():
        @pl.when(inside.cond)
        def _():
            l_lanes[0].start()
            arrived(k_l, s_ly.at[0])
            l_lanes[1].start()
            arrived(k_l, s_ly.at[1])
            ref = lg.at[1 - yh, 2 * x + 1 - yl]
            sends.go(ref, ref, s_ly.at[2], pair, k_l, inside)
            l_lanes[2].start()
            arrived(k_l, s_ly.at[2])
            l_lanes[3].start()

    def mids(lanes):
        @pl.when(inside.cond)
        def _():
            for lane in lanes:
                lane.mid(0)
                lane.mid(1)

    def ends(lanes):
        @pl.when(inside.cond)
        def _():
            for lane in lanes:
                lane.end()

    def from_sibling(buf, sems):
        @pl.when(outside.cond)
        def _():
            for u in range(2):
                for v in range(8):
                    arrived(buf.at[u, v], sems.at[u, v])

    def y_sib(u, v):
        ref = yg.at[u, v]
        sends.go(ref, ref, s_ysib.at[u, v], sib, k_l, inside)

    y_lanes = [
        ring_x(yg, s_yx, y_sib, 0, 0, yl),
        ring_x(yg, s_yx, y_sib, 1, 1, yl),
        ring_x(yg, s_yx, y_sib, 2, 0, 1 - yl),
        ring_x(yg, s_yx, y_sib, 3, 1, 1 - yl),
    ]

    def y_own_start():
        @pl.when(inside.cond)
        def _():
            for u in range(2):
                ref = yg.at[u, own_v]
                sends.go(ref, ref, s_yy.at[u], pair, k_l, inside)
            y_lanes[0].start()
            y_lanes[1].start()

    def y_pair_start():
        @pl.when(inside.cond)
        def _():
            for u in range(2):
                arrived(k_l, s_yy.at[u])
                y_lanes[2 + u].start()

    def c_at(at, yy):
        return 8 * at + 4 * yy + 2 * core

    def c_sib(at, yy):
        ref = rc.at[pl.ds(c_at(at, yy), 2)]
        sends.go(ref, ref, s_csib.at[2 * at + yy], sib, k_c)

    c_lanes = [
        Ring4(
            sends, lambda at, yy=yy: rc.at[pl.ds(c_at(at, yy), 2)], lambda at, h, yy=yy: rc.at[c_at(at, yy) + h], x,
            xp, xm, s_cx, k_c, k_ch, lane, sib=lambda at, yy=yy: c_sib(at, yy),
        )
        for lane, yy in enumerate((yl, 1 - yl))
    ]

    def zsum(t, slots, sems):
        def part(step, side):
            if step == 0:
                d = up(z, 4, Z)
                ref, dst = t.at[d, pl.ds(H * side, H)], slots.at[side, 0, pl.ds(0, H)]
                kind = slots.at[side, 0, pl.ds(0, H)]
            else:
                d = up(z, 4 - step, Z) if side == 0 else up(z, 4 + step, Z)
                ref, dst = t.at[d], slots.at[side, step]
                kind = dst
            return d, ref, dst, kind

        def add(step, side, d):
            if step == 0:
                got = slots.at[side, 0, pl.ds(0, H)]
                arrived(got, sems.at[side, 0])
                t[pl.ds(d, 1), pl.ds(H * side, H)] += got[...].reshape(1, H, N)
            else:
                got = slots.at[side, step]
                arrived(got, sems.at[side, step])
                t[pl.ds(d, 1)] += got[...].reshape(1, N, N)

        def step(n):
            for side in range(2):
                d, ref, dst, kind = part(n, side)
                if n > 0:
                    add(n - 1, side, d)
                sends.go(ref, dst, sems.at[side, n], zp if side == 0 else zm, kind)

        def last():
            arrived(slots.at[0, 3], sems.at[0, 3])
            arrived(slots.at[1, 3], sems.at[1, 3])
            d = jnp.int32(1) * z
            return t[pl.ds(d, 1)].reshape(N, N) + slots[0, 3] + slots[1, 3]

        return step, last

    root_step, root_last = zsum(troot, rsr, s_zr)
    child_step, child_last = zsum(tchild, rsc, s_zc)

    def transposed(dst, blocks):
        for u in range(2):
            t = blocks(u).T
            hi, lo = split(t)
            dst[0, :, N * u : N * u + N] = hi
            dst[1, :, N * u : N * u + N] = lo

    def root_term(d):
        q = 2 * (2 * d + yh)
        rows = [
            jnp.concatenate(
                [rg[u, pl.ds(q, 1)].reshape(N, H), rg[u, pl.ds(q + 1, 1)].reshape(N, H)], axis=1
            )
            for u in range(2)
        ]
        troot[pl.ds(d, 1)] = dot3(rjt[0], rjt[1], jnp.concatenate(rows, axis=0)).reshape(1, N, N)

    def grown(buf, left, d):
        both = jnp.concatenate([buf[u, pl.ds(d, 1)].reshape(N, N) for u in range(2)], axis=0)
        return dot3(left[0], left[1], both).reshape(1, N, N)

    def panel_pair(f):
        return pg[pl.ds(2 * f, 2)].reshape(N, N)

    def picked(buf, f):
        return jnp.concatenate([buf(st[2 * f]), buf(st[2 * f + 1])], axis=1)

    first.start()
    second[0].start()
    sends.go(pg.at[row], pg.at[row], s_pw.at[0], yo, pg.at[0])
    p_start(0)
    first.mid(0)
    second[1].start()
    first.mid(1)
    second[2].start()
    l_y_start()
    arrived(pg.at[p_slot(1, z)], s_pw.at[0])
    p_start(1)
    p_step(0, 1)
    second[0].mid(0)
    second[0].mid(1)
    first.end()
    second[3].start()
    p_step(1, 1)
    p_step(0, 2)
    second[1].mid(0)
    second[1].mid(1)
    p_step(1, 2)
    p_step(0, 3)
    second[2].mid(0)
    second[2].mid(1)
    p_step(1, 3)
    second[3].mid(0)
    second[3].mid(1)
    l_x_start()
    for k in range(4):
        second[k].end()
    for n in range(16):
        arrived(k_r, s_rsib.at[n])

    mine = 2 * col
    transposed(rjt, lambda u: jnp.concatenate(
        [rg[u, pl.ds(mine, 1)].reshape(N, H), rg[u, pl.ds(mine + 1, 1)].reshape(N, H)], axis=1))

    def root_body(n, carry):
        root_term(up(z, 4 + n, Z))
        return carry

    lax.fori_loop(0, 1, root_body, 0)
    root_step(0)
    lax.fori_loop(1, Z, root_body, 0)
    mids(l_lanes)
    root_step(1)
    p_end(0)
    p_end(1)

    for u in range(2):
        def y_body(f, acc, u=u):
            lhs = picked(lambda s: rg[u, s], f)
            hi, lo = split(lhs)
            return acc + dot3(hi, lo, panel_pair(f))

        yj[u] = lax.fori_loop(0, F // 2, y_body, jnp.zeros((N, N), F32))

    @pl.when(inside.cond)
    def _():
        for u in range(2):
            yg[u, pl.ds(own_v, 1)] = yj[u].reshape(1, N, N)

    y_own_start()
    ends(l_lanes)
    root_step(2)

    @pl.when(outside.cond)
    def _():
        arrived(k_l, s_lj.at[0])

    @pl.when(inside.cond)
    def _():
        lj[pl.ds(1 - yh, 1)] = lg[1 - yh, pl.ds(own_v, 1)]

    transposed(ljt, lambda u: lj[u])
    transposed(yjt, lambda u: yj[u])
    y_pair_start()
    from_sibling(lg, s_lsib)

    def child_l(n, carry):
        tchild[pl.ds(n, 1)] = grown(lg, ljt, n)
        return carry

    root_step(3)
    mids(y_lanes[:2])
    lax.fori_loop(0, Z, child_l, 0)
    mids(y_lanes[2:])
    done = root_last().T
    root[...] = done
    rc[pl.ds(mine, 1)] = done[:, 0:H].reshape(1, N, H)
    rc[pl.ds(mine + 1, 1)] = done[:, H:N].reshape(1, N, H)
    c_pair = rc.at[pl.ds(mine, 2)]
    sends.go(c_pair, c_pair, s_cy.at[0], pair, k_c)
    c_lanes[0].start()
    ends(y_lanes)
    from_sibling(yg, s_ysib)

    def child_y(n, carry):
        d = up(z, 4 + n, Z)
        tchild[pl.ds(d, 1)] += grown(yg, yjt, d)
        return carry

    lax.fori_loop(0, 1, child_y, 0)
    child_step(0)
    arrived(k_c, s_cy.at[0])
    c_lanes[1].start()
    lax.fori_loop(1, Z, child_y, 0)
    c_lanes[0].mid(0)
    c_lanes[0].mid(1)
    child_step(1)
    c_lanes[1].mid(0)
    c_lanes[1].mid(1)
    c_lanes[0].end()
    c_lanes[1].end()
    child_step(2)
    for n in range(8):
        arrived(k_c, s_csib.at[n])

    def cross_body(f, acc):
        lhs = picked(lambda s: rc[s], f)
        hi, lo = split(lhs)
        return acc + dot3(hi, lo, panel_pair(f))

    acc = lax.fori_loop(0, F // 2, cross_body, jnp.zeros((N, N), F32))
    for h in range(2):
        live = jnp.int32(0)
        for f in range(F):
            live += (st[f] == 2 * row + h).astype(jnp.int32)
        cross[H * h : H * h + H, :] = acc[H * h : H * h + H, :] * (-live.astype(F32))
    child_step(3)
    child[...] = child_last().T
    sends.drain()


def shards(root_inv, child_inv, child_panel, structure):
    vmem = pl.BlockSpec(memory_space=pltpu.VMEM)
    dma = pltpu.SemaphoreType.DMA
    out = jax.ShapeDtypeStruct((N, N), F32)
    call = pl.pallas_call(
        kernel,
        out_shape=(out, out, out),
        in_specs=[pl.BlockSpec(memory_space=pltpu.SMEM), vmem, vmem, vmem],
        out_specs=(vmem, vmem, vmem),
        scratch_shapes=[
            pltpu.VMEM((2, 32, N, H), F32),
            pltpu.VMEM((2, Z, N, N), F32),
            pltpu.VMEM((2, Z, N, N), F32),
            pltpu.VMEM((2, N, N), F32),
            pltpu.VMEM((2, N, N), F32),
            pltpu.VMEM((32, N, H), F32),
            pltpu.VMEM((F, H, N), F32),
            pltpu.VMEM((2, N, 2 * N), BF16),
            pltpu.VMEM((2, N, 2 * N), BF16),
            pltpu.VMEM((2, N, 2 * N), BF16),
            pltpu.VMEM((Z, N, N), F32),
            pltpu.VMEM((Z, N, N), F32),
            pltpu.VMEM((2, 4, N, N), F32),
            pltpu.VMEM((2, 4, N, N), F32),
            dma((200,)),
            dma((1, 4)), dma((4, 4)), dma((16,)),
            dma((1,)), dma((3,)), dma((4, 4)), dma((2, 8)),
            dma((2,)), dma((4, 4)), dma((2, 8)),
            dma((1,)), dma((2, 4)), dma((8,)),
            dma((2, 2, 4)), dma((1,)),
            dma((2, 4)), dma((2, 4)),
        ],
        compiler_params=pltpu.CompilerParams(
            collective_id=0, has_side_effects=True, vmem_limit_bytes=56 * 2**20
        ),
    )
    return call(structure, root_inv, child_inv, child_panel)


def solution(mesh):
    placed = (P("prow", "pcol"), P("prow", "pcol"), P("prow", "pcol"), P())
    return jax.shard_map(
        shards,
        mesh=mesh,
        in_specs=placed,
        out_specs=(P("prow", "pcol"), P("prow", "pcol"), P("prow", "pcol")),
        check_vma=False,
    )
```

time: 925 us -> 120 us (0.13)
  waiting for transfers between devices: 855 us -> 0 us
  Pallas kernels: 0 us -> 115 us
  matrix products: 44.8 us -> 0 us
  between operations: 14.2 us -> 0.65 us
    reduce_scatter x3 -> x0, waiting for transfers between devices: 622 us -> none  [the longest x1 214 us: shards(): lax.psum_scatter(update_terms, 'prow', scatter_dimension=0, tiled=True)]
    all_gather x5 -> x0, waiting for transfers between devices: 231 us -> none  [the longest x1 86.5 us: shards(): gathered_rows = lax.all_gather(child_panel, 'prow', axis=0, tiled=True)]
    pallas_call x0 -> x1, Pallas kernels: none -> 115 us  [shards(): return call(structure, root_inv, child_inv, child_panel)]
    dot_general x5 -> x0, matrix products: 44.8 us -> none  [product(): jnp.einsum(subscripts, former, latter, precision=lax.Precision.HIGHEST, p...]
  transfers between devices with their start and end apart: 8 -> 0, of which waited for: 8 -> 0; matrix products, arithmetic and copies ran while one was open for 4% -> 0% of each run, Pallas kernels for 0% -> 0%
where the time goes in v1:
time: 120 us
  Pallas kernels  115 us (96%)
  local copies, waits for them, and re-layouts  3.46 us (3%)
    pallas_call x1, Pallas kernels, shards(): return call(structure, root_inv, child_inv, child_panel)  115 us
    unnamed x7, local copies, waits for them, and re-layouts  3.46 us

profile of v1, /device:TPU:1, one launch (start us, length us, event | category | flops | bytes accessed | tf_op | source)
XLA Modules:
  0.0 119.5 jit_solution(206807377301023378)
XLA Ops:
  0.6 115.4 %shard_map.67 = (f32[256,256]{1,0:T(8,128)}, f32[256,256]{1,0:T(8,128)}, f32[256,256]{1,0:T(8,128)}) custom-call(s32[16]{0:T(128)} %st.1, f32[256,256]{1,0:T(8,128)} %r.1, f32[256,256]{1,0:T(8,128)} %l.1, f32[128,256]{1,0:T(8,128)} %p.1), custom_call_target="tpu_custom_call" | custom-call | tf_op jit(solution)/shard_map/pallas_call | solution.py:541
  116.0 0.0 copy-start.1
  116.1 1.7 %copy.10 = f32[256,256]{1,0:T(8,128)} copy(f32[256,256]{1,0:T(8,128)} %get-tuple-element.6) | data formatting | bytes 524288
  117.8 0.0 copy-done.1
  117.8 0.0 copy-start
  117.8 0.7 copy.11
  118.5 0.3 copy-done
  118.8 0.7 copy.12
Async XLA Ops:
  116.0 1.7 %copy-start.1 = (f32[256,256]{1,0:T(8,128)S(1)}, f32[256,256]{1,0:T(8,128)}, u32[]{:S(2)}) copy-start(f32[256,256]{1,0:T(8,128)} %get-tuple-element.7) | copy-start | bytes 786436
  117.8 1.0 copy-start

commit v2 on v0

v2 whole, which is shorter than its diff:
```python
import jax
import jax.numpy as jnp
from jax import lax
from jax.experimental import pallas as pl
from jax.experimental.pallas import tpu as pltpu
from jax.sharding import PartitionSpec as P

MESH = pl.DeviceIdType.MESH
F32 = jnp.float32
BF16 = jnp.bfloat16
F = 16
N = 256
H = 128
Z = 8
R4 = 4


def split(v):
    hi = v.astype(BF16)
    return hi, (v - hi.astype(F32)).astype(BF16)


def dot3(a_hi, a_lo, b):
    b_hi, b_lo = split(b)
    out = jnp.dot(a_hi, b_hi, preferred_element_type=F32)
    out += jnp.dot(a_hi, b_lo, preferred_element_type=F32)
    return out + jnp.dot(a_lo, b_hi, preferred_element_type=F32)


def up(v, by, n):
    return lax.rem(v + by, n)


def arrived(ref, sem):
    pltpu.make_async_copy(ref, ref, sem).wait()


class Cond:
    def __init__(self, cond):
        self.cond = cond

    def __call__(self, body):
        pl.when(self.cond)(body)


class Sends:
    def __init__(self, sem):
        self.sem, self.count, self.open = sem, 0, []

    def go(self, src, dst, recv, dev, kind, when=None):
        pltpu.make_async_remote_copy(
            src_ref=src, dst_ref=dst, send_sem=self.sem.at[self.count], recv_sem=recv, device_id=dev, device_id_type=MESH
        ).start()
        self.open.append((self.count, kind, when))
        self.count += 1

    def drain(self):
        for when in dict.fromkeys(w for _, _, w in self.open):
            def body(when=when):
                for n, kind, w in self.open:
                    if w is when:
                        arrived(kind, self.sem.at[n])
            if when is None:
                body()
            else:
                when(body)


class Ring4:
    def __init__(self, sends, ref, half, pos, plus, minus, sems, kind, kind_half, got, when=None):
        self.__dict__.update(locals())
        self.places = (pos, up(pos, 3, R4), up(pos, 1, R4), up(pos, 2, R4))

    def start(self):
        ref = self.ref(self.pos)
        self.sends.go(ref, ref, self.sems.at[0], self.plus, self.kind, self.when)
        self.sends.go(ref, ref, self.sems.at[1], self.minus, self.kind, self.when)
        self.got(self.pos, 0)

    def mid(self, side):
        at = self.places[1 + side]
        arrived(self.ref(at), self.sems.at[side])
        ref = self.half(at, side)
        self.sends.go(ref, ref, self.sems.at[2 + side], (self.plus, self.minus)[side], self.kind_half, self.when)
        self.got(at, 1 + side)

    def mids(self):
        self.mid(0)
        self.mid(1)

    def end(self):
        at = self.places[3]
        arrived(self.half(at, 0), self.sems.at[2])
        arrived(self.half(at, 1), self.sems.at[3])
        self.got(at, 3)


def kernel(
    st, r, l, p, root, cross, child,
    rg, rc, ro, lsame, lother, ysame, yother, oth_r, oth_l, oth_y, yown, lown, pg, jt_r, jt_l, jt_y, troot, tchild, rsr, rsc,
    s_send,
    s_rx, s_rp, s_rs, s_cx, s_cp, s_cs,
    s_rox, s_roy, s_ros, s_roo,
    s_lx, s_lox, s_ly, s_lp, s_ls, s_lo,
    s_yx, s_yox, s_yy, s_yp, s_ys, s_yo,
    s_p, s_pw, s_zr, s_zc,
):
    row, col = lax.axis_index("prow"), lax.axis_index("pcol")
    z, yh = lax.div(row, 2), lax.rem(row, 2)
    x, yl, core = lax.div(col, 4), lax.rem(lax.div(col, 2), 2), lax.rem(col, 2)
    y = 2 * yh + yl
    yn = 1 - yl

    def dev(zz, yy, xx, cc):
        return (2 * zz + lax.div(yy, 2), 4 * xx + 2 * lax.rem(yy, 2) + cc)

    xp, xm = dev(z, y, up(x, 1, 4), core), dev(z, y, up(x, 3, 4), core)
    zp, zm = dev(up(z, 1, Z), y, x, core), dev(up(z, 7, Z), y, x, core)
    sib = dev(z, y, x, 1 - core)
    yo = dev(z, up(y, 2, 4), x, core)
    pair = dev(z, 2 * yh + yn, x, core)
    cross_y = dev(z, 2 * (1 - yh) + yn, x, core)

    barrier = pltpu.get_barrier_semaphore()
    for d in (xp, xm, pair, cross_y, zp, zm, sib, yo):
        pl.semaphore_signal(barrier, inc=1, device_id=d, device_id_type=MESH)

    inside = Cond(core == yh)
    outside = Cond(core != yh)
    sends = Sends(s_send)
    v0, v1 = 2 * x + yl, 2 * x + yn

    for h in range(2):
        rg[pl.ds(2 * col + h, 1)] = r[:, H * h : H * h + H].reshape(1, N, H)
        lown[h] = l[:, H * h : H * h + H]
    pg[pl.ds(row, 1)] = p[...].reshape(1, H, N)

    @inside
    def _():
        for h in range(2):
            lsame[pl.ds(v0, 1), h] = l[:, H * h : H * h + H].reshape(1, N, H)

    pl.semaphore_wait(barrier, 8)

    k_2, k_1, k_h = rg.at[pl.ds(0, 2)], rg.at[0], rg.at[0, pl.ds(0, H)]

    class Row:
        def __init__(self, buf, s_x, s_pair, s_sib):
            self.buf, self.s_x, self.s_pair, self.s_sib = buf, s_x, s_pair, s_sib

            def lane(n, yy, h, pairing):
                return Ring4(
                    sends, lambda at: buf.at[self.slot(at, yy, h)],
                    lambda at, q: buf.at[self.slot(at, yy, h), pl.ds(H * q, H)],
                    x, xp, xm, s_x.at[n], k_1, k_h, lambda at, k: self.got(at, yy, h, k, pairing),
                )

            self.lanes = [lane(0, yl, 0, True), lane(1, yl, 1, False), lane(2, yn, 1, False)]

        def slot(self, at, yy, h):
            return 8 * at + 4 * yy + 2 * core + h

        def got(self, at, yy, h, k, pairing):
            ref = self.buf.at[self.slot(at, yy, h)]
            if pairing:
                sends.go(ref, ref, self.s_pair.at[k], pair, k_1)
            sends.go(ref, ref, self.s_sib.at[at, yy, h], sib, k_1)

        def start(self):
            own = self.buf.at[self.slot(x, yl, 1)]
            sends.go(own, own, self.s_pair.at[4], pair, k_1)
            self.lanes[0].start()
            self.lanes[1].start()

        def pair_in(self):
            arrived(k_1, self.s_pair.at[4])
            self.lanes[2].start()

        def pairs(self, ks):
            for k in ks:
                arrived(k_1, self.s_pair.at[k])
                self.got(self.lanes[0].places[k], yn, 0, k, False)

        def finish(self):
            for n in range(16):
                arrived(k_1, self.s_sib.at[n // 4, n // 2 % 2, n % 2])

    class Plane:
        def __init__(self, own, same, other, oth, s_x, s_ox, s_y, s_pair, s_sib, s_oth, units):
            self.own, self.same, self.other, self.oth = own, same, other, oth
            self.s_y, self.s_pair, self.s_sib, self.s_oth = s_y, s_pair, s_sib, s_oth
            self.units = units

            def lane(buf, which, yy, c, sems, pairing):
                return Ring4(
                    sends, lambda at: self.unit(buf, 2 * at + yy, c), lambda at, q: self.half(buf, 2 * at + yy, c, q),
                    x, xp, xm, sems, self.kind(), self.kind_half(),
                    lambda at, k: self.got(buf, which, 2 * at + yy, c, k, pairing), inside,
                )

            self.inner = [lane(same, 0, yl, c, s_x.at[c], True) for c in range(units)] if same is not None else []
            self.outer = [
                [lane(other, 1, yl, c, s_ox.at[c, 0], False), lane(other, 1, yn, c, s_ox.at[c, 1], False)]
                for c in range(units)
            ]

        def kind(self):
            return k_1 if self.units == 2 else k_2

        def kind_half(self):
            return k_h if self.units == 2 else k_1

        def unit(self, buf, v, c):
            return buf.at[v, c] if self.units == 2 else buf.at[v]

        def half(self, buf, v, c, q):
            return buf.at[v, c, pl.ds(H * q, H)] if self.units == 2 else buf.at[v, q]

        def got(self, buf, which, v, c, k, pairing):
            ref = self.unit(buf, v, c)
            if pairing:
                sends.go(ref, ref, self.s_pair.at[c, k], pair, self.kind(), inside)
            sends.go(ref, ref, self.s_sib.at[which, c, v], sib, self.kind(), inside)

        def src(self, c):
            return self.own.at[c] if self.units == 2 else self.own

        def start(self, c):
            @inside
            def _():
                if self.inner:
                    self.inner[c].start()
                if c == self.units - 1:
                    sends.go(self.own, self.oth, self.s_oth.at[0], yo, k_2, inside)

            @outside
            def _():
                ref = self.unit(self.other, v0, c)
                sends.go(self.src(c), ref, self.s_y.at[c, 0], yo, self.kind(), outside)
                sends.go(self.src(c), ref, self.s_y.at[c, 1], cross_y, self.kind(), outside)

        def outer_start(self, c):
            @inside
            def _():
                for n in range(2):
                    arrived(self.kind(), self.s_y.at[c, n])
                    self.outer[c][n].start()

        def inner_mid(self, c):
            @inside
            def _():
                self.inner[c].mids()

        def inner_end(self, c):
            @inside
            def _():
                self.inner[c].end()

        def outer_mid(self, c):
            @inside
            def _():
                for lane in self.outer[c]:
                    lane.mids()

        def outer_end(self, c):
            @inside
            def _():
                for lane in self.outer[c]:
                    lane.end()

        def pairs(self, c, ks):
            @inside
            def _():
                for k in ks:
                    arrived(self.kind(), self.s_pair.at[c, k])
                    self.got(self.same, 0, 2 * self.inner[c].places[k] + yn, c, k, False)

        def finish(self, c):
            @outside
            def _():
                for v in range(8):
                    if self.inner:
                        arrived(self.kind(), self.s_sib.at[0, c, v])
                    arrived(self.kind(), self.s_sib.at[1, c, v])

        def other_own(self):
            @outside
            def _():
                arrived(k_2, self.s_oth.at[0])

            @inside
            def _():
                self.oth[...] = self.other[pl.ds(v0, 1)].reshape(2, N, H)

    rr = Row(rg, s_rx, s_rp, s_rs)
    cc = Row(rc, s_cx, s_cp, s_cs)
    r_own = rg.at[pl.ds(2 * col, 2)]
    ra = Plane(r_own, None, ro, oth_r, None, s_rox, s_roy, None, s_ros, s_roo, 1)
    la = Plane(lown, lsame, lother, oth_l, s_lx, s_lox, s_ly, s_lp, s_ls, s_lo, 2)
    ya = Plane(yown, ysame, yother, oth_y, s_yx, s_yox, s_yy, s_yp, s_ys, s_yo, 2)

    def p_slot(lane, zz):
        return 2 * zz + (yh if lane == 0 else 1 - yh)

    def p_push(lane, zz, step, side):
        n = p_slot(lane, zz)
        if step < 3:
            ref, kind = pg.at[n], pg.at[0]
        else:
            ref, kind = pg.at[n, pl.ds(64 * side, 64)], pg.at[0, pl.ds(0, 64)]
        sends.go(ref, ref, s_p.at[lane, side, step], zp if side == 0 else zm, kind)

    def p_start(lane):
        p_push(lane, z, 0, 0)
        p_push(lane, z, 0, 1)

    def p_step(lane, step):
        for side in range(2):
            zz = up(z, Z - step, Z) if side == 0 else up(z, step, Z)
            arrived(pg.at[p_slot(lane, zz)], s_p.at[lane, side, step - 1])
            p_push(lane, zz, step, side)

    def p_end(lane):
        n = p_slot(lane, up(z, 4, Z))
        for side in range(2):
            arrived(pg.at[n, pl.ds(64 * side, 64)], s_p.at[lane, side, 3])

    class Sum:
        def __init__(self, t, slots, sems):
            self.t, self.slots, self.sems = t, slots, sems

        def add(self, side, n, c, d):
            got = self.slots.at[side, n, c]
            arrived(got, self.sems.at[side, n, c])
            self.t[pl.ds(d, 1), c] += got[...].reshape(1, N, H)

        def step(self, n, c):
            for side in (c, 1 - c):
                if n == 0 and side != c:
                    continue
                d = up(z, 4 - n, Z) if side == 0 else up(z, 4 + n, Z)
                if n > 1 or (n == 1 and side == c):
                    self.add(side, n - 1, c, d)
                sends.go(
                    self.t.at[d, c], self.slots.at[side, n, c], self.sems.at[side, n, c], zp if side == 0 else zm,
                    self.slots.at[0, 0, 0],
                )

        def last(self, c):
            arrived(self.slots.at[0, 3, c], self.sems.at[0, 3, c])
            arrived(self.slots.at[1, 3, c], self.sems.at[1, 3, c])
            return self.t[pl.ds(z, 1), c].reshape(N, H) + self.slots[0, 3, c] + self.slots[1, 3, c]

    zr, zc = Sum(troot, rsr, s_zr), Sum(tchild, rsc, s_zc)

    def left(dst, same, oth):
        for u, blk in enumerate((same, oth)):
            for h in range(2):
                hi, lo = split(blk(h).T)
                dst[0, H * h : H * h + H, N * u : N * u + N] = hi
                dst[1, H * h : H * h + H, N * u : N * u + N] = lo

    def term(t, jt, same, oth, m, c, add):
        d = (up(z, 4 + m, Z), up(z, 8 - m if m else 0, Z) if m == 0 else up(z, 4 - m, Z))
        cols = [
            jnp.concatenate([same(e, c), oth(e, c)], axis=0) for e in d
        ]
        out = dot3(jt[0], jt[1], jnp.concatenate(cols, axis=1))
        for n, e in enumerate(d):
            new = out[:, H * n : H * n + H].reshape(1, N, H)
            if add:
                t[pl.ds(e, 1), c] += new
            else:
                t[pl.ds(e, 1), c] = new

    def root_term(m, c):
        term(
            troot, jt_r, lambda e, c: rg[pl.ds(4 * e + 2 * yh + c, 1)].reshape(N, H),
            lambda e, c: ro[pl.ds(e, 1), c].reshape(N, H), m, c, False,
        )

    def child_term(same, other, jt, m, c, add):
        term(
            tchild, jt, lambda e, c: same[pl.ds(e, 1), c].reshape(N, H),
            lambda e, c: other[pl.ds(e, 1), c].reshape(N, H), m, c, add,
        )

    def panel_product(buf):
        def body(f, acc):
            lhs = jnp.concatenate([buf[st[2 * f]], buf[st[2 * f + 1]]], axis=1)
            hi, lo = split(lhs)
            return acc + dot3(hi, lo, pg[pl.ds(2 * f, 2)].reshape(N, N))

        return lax.fori_loop(0, F // 2, body, jnp.zeros((N, N), F32))

    rr.start()
    sends.go(pg.at[row], pg.at[row], s_pw.at[0], yo, pg.at[0])
    p_start(0)
    ra.start(0)
    rr.pair_in()
    rr.lanes[0].mids()
    arrived(pg.at[p_slot(1, z)], s_pw.at[0])
    p_start(1)
    p_step(0, 1)
    rr.lanes[1].mids()
    p_step(1, 1)
    rr.lanes[2].mids()
    p_step(0, 2)
    la.start(0)
    la.start(1)
    rr.pairs((0,))
    rr.lanes[0].end()
    p_step(1, 2)
    rr.lanes[1].end()
    rr.lanes[2].end()
    ra.outer_start(0)
    p_step(0, 3)
    rr.pairs((1, 2, 3))
    p_step(1, 3)
    rr.finish()
    p_end(0)
    p_end(1)

    y_new = panel_product(rg)
    for h in range(2):
        yown[h] = y_new[:, H * h : H * h + H]

    @inside
    def _():
        for h in range(2):
            ysame[pl.ds(v0, 1), h] = yown[h].reshape(1, N, H)

    ya.start(0)
    ya.start(1)
    ra.outer_mid(0)
    la.inner_mid(0)
    la.inner_mid(1)
    ra.outer_end(0)
    ra.finish(0)
    ra.other_own()
    left(jt_r, lambda h: rg[pl.ds(2 * col + h, 1)].reshape(N, H), lambda h: oth_r[h])
    root_term(0, 0)
    zr.step(0, 0)
    root_term(0, 1)
    zr.step(0, 1)
    root_term(1, 1)
    root_term(1, 0)
    la.outer_start(0)
    la.outer_start(1)
    zr.step(1, 0)
    zr.step(1, 1)
    ya.outer_start(0)
    ya.inner_mid(0)
    ya.inner_mid(1)
    ya.outer_start(1)
    for m in (2, 3):
        for c in range(2):
            root_term(m, c)
    la.inner_end(0)
    la.inner_end(1)
    la.outer_mid(0)
    la.outer_mid(1)
    zr.step(2, 0)
    zr.step(2, 1)
    ya.outer_mid(0)
    ya.outer_mid(1)
    ya.inner_end(0)
    ya.inner_end(1)
    la.pairs(0, range(4))
    la.pairs(1, range(4))
    la.outer_end(0)
    la.outer_end(1)
    la.finish(0)
    la.finish(1)
    la.other_own()
    left(jt_l, lambda h: lown[h], lambda h: oth_l[h])
    zr.step(3, 0)
    zr.step(3, 1)
    ya.pairs(0, range(4))
    ya.pairs(1, range(4))
    for c in range(2):
        for m in range(4):
            child_term(lsame, lother, jt_l, m, c, False)
    for c in range(2):
        done = zr.last(c).T
        root[H * c : H * c + H, :] = done
        for h in range(2):
            rc[pl.ds(2 * col + h, 1), H * c : H * c + H] = done[:, H * h : H * h + H].reshape(1, H, H)
    cc.start()
    ya.outer_end(0)
    ya.outer_end(1)
    ya.finish(0)
    ya.finish(1)
    ya.other_own()
    left(jt_y, lambda h: yown[h], lambda h: oth_y[h])
    for c in range(2):
        child_term(ysame, yother, jt_y, 0, c, True)
        zc.step(0, c)
    cc.pair_in()
    for c in range(2):
        child_term(ysame, yother, jt_y, 1, 1 - c, True)
    cc.lanes[0].mids()
    cc.lanes[1].mids()
    zc.step(1, 0)
    zc.step(1, 1)
    for m in (2, 3):
        for c in range(2):
            child_term(ysame, yother, jt_y, m, c, True)
    cc.lanes[2].mids()
    cc.lanes[0].end()
    cc.pairs((0, 1, 2))
    zc.step(2, 0)
    zc.step(2, 1)
    cc.lanes[1].end()
    cc.lanes[2].end()
    cc.pairs((3,))
    zc.step(3, 0)
    zc.step(3, 1)
    cc.finish()

    acc = panel_product(rc)
    for h in range(2):
        live = jnp.int32(0)
        for f in range(F):
            live += (st[f] == 2 * row + h).astype(jnp.int32)
        cross[H * h : H * h + H, :] = acc[H * h : H * h + H, :] * (-live.astype(F32))
    for c in range(2):
        child[H * c : H * c + H, :] = zc.last(c).T
    sends.drain()


def copies(a, b, c, ao, bo, co, sem):
    moves = [pltpu.make_async_copy(s, d, sem.at[n]) for n, (s, d) in enumerate(((a, ao), (b, bo), (c, co)))]
    for move in moves:
        move.start()
    for move in moves:
        move.wait()


def shards(root_inv, child_inv, child_panel, structure):
    vmem = pl.BlockSpec(memory_space=pltpu.VMEM)
    hbm = pl.BlockSpec(memory_space=pl.ANY)
    dma = pltpu.SemaphoreType.DMA
    out = jax.ShapeDtypeStruct((N, N), F32)
    half = (2, N, H)
    plane = [dma((2, 4)), dma((2, 2, 4)), dma((2, 2)), dma((2, 4)), dma((2, 2, 8)), dma((1,))]
    line = [dma((3, 4)), dma((5,)), dma((4, 2, 2))]
    call = pl.pallas_call(
        kernel,
        out_shape=(out, out, out),
        in_specs=[pl.BlockSpec(memory_space=pltpu.SMEM), vmem, vmem, vmem],
        out_specs=(vmem, vmem, vmem),
        scratch_shapes=[
            pltpu.VMEM((32, N, H), F32),
            pltpu.VMEM((32, N, H), F32),
            pltpu.VMEM((Z,) + half, F32),
            pltpu.VMEM((Z,) + half, F32),
            pltpu.VMEM((Z,) + half, F32),
            pltpu.VMEM((Z,) + half, F32),
            pltpu.VMEM((Z,) + half, F32),
            pltpu.VMEM(half, F32),
            pltpu.VMEM(half, F32),
            pltpu.VMEM(half, F32),
            pltpu.VMEM(half, F32),
            pltpu.VMEM(half, F32),
            pltpu.VMEM((F, H, N), F32),
            pltpu.VMEM((2, N, 2 * N), BF16),
            pltpu.VMEM((2, N, 2 * N), BF16),
            pltpu.VMEM((2, N, 2 * N), BF16),
            pltpu.VMEM((Z,) + half, F32),
            pltpu.VMEM((Z,) + half, F32),
            pltpu.VMEM((2, 4) + half, F32),
            pltpu.VMEM((2, 4) + half, F32),
            dma((320,)),
            *line,
            *line,
            dma((1, 2, 4)), dma((1, 2)), dma((2, 1, 8)), dma((1,)),
            *plane,
            *plane,
            dma((2, 2, 4)), dma((1,)),
            dma((2, 4, 2)), dma((2, 4, 2)),
        ],
        compiler_params=pltpu.CompilerParams(
            collective_id=0, has_side_effects=True, vmem_limit_bytes=56 * 2**20
        ),
    )
    parts = call(structure, root_inv, child_inv, child_panel)
    return pl.pallas_call(
        copies,
        out_shape=(out, out, out),
        in_specs=[hbm] * 3,
        out_specs=(hbm, hbm, hbm),
        scratch_shapes=[dma((3,))],
    )(*parts)


def solution(mesh):
    placed = (P("prow", "pcol"), P("prow", "pcol"), P("prow", "pcol"), P())
    return jax.shard_map(
        shards,
        mesh=mesh,
        in_specs=placed,
        out_specs=(P("prow", "pcol"), P("prow", "pcol"), P("prow", "pcol")),
        check_vma=False,
    )
```

time: 925 us -> 146 us (0.16)
  waiting for transfers between devices: 855 us -> 0 us
  Pallas kernels: 0 us -> 145 us
  matrix products: 44.8 us -> 0 us
  between operations: 14.2 us -> 0.64 us
    reduce_scatter x3 -> x0, waiting for transfers between devices: 622 us -> none  [the longest x1 214 us: shards(): lax.psum_scatter(update_terms, 'prow', scatter_dimension=0, tiled=True)]
    all_gather x5 -> x0, waiting for transfers between devices: 231 us -> none  [the longest x1 86.5 us: shards(): gathered_rows = lax.all_gather(child_panel, 'prow', axis=0, tiled=True)]
    pallas_call x0 -> x2, Pallas kernels: none -> 145 us  [the longest x1 120 us: shards(): parts = call(structure, root_inv, child_inv, child_panel)]
    dot_general x5 -> x0, matrix products: 44.8 us -> none  [product(): jnp.einsum(subscripts, former, latter, precision=lax.Precision.HIGHEST, p...]
  transfers between devices with their start and end apart: 8 -> 0, of which waited for: 8 -> 0; matrix products, arithmetic and copies ran while one was open for 4% -> 0% of each run, Pallas kernels for 0% -> 0%
where the time goes in v2:
time: 146 us
  Pallas kernels  145 us (99%)
    pallas_call x1, Pallas kernels, shards(): parts = call(structure, root_inv, child_inv, child_panel)  120 us
    pallas_call x1, Pallas kernels, shards(): pl.pallas_call(copies, out_shape=(out, out, out), in_specs=[hbm] * 3, out...  25 us

profile of v2, /device:TPU:1, one launch (start us, length us, event | category | flops | bytes accessed | tf_op | source)
XLA Modules:
  0.0 145.7 jit_solution(433851750574087669)
XLA Ops:
  0.6 120.1 %shard_map.67 = (f32[256,256]{1,0:T(8,128)}, f32[256,256]{1,0:T(8,128)}, f32[256,256]{1,0:T(8,128)}) custom-call(s32[16]{0:T(128)} %st.1, f32[256,256]{1,0:T(8,128)} %r.1, f32[256,256]{1,0:T(8,128)} %l.1, f32[128,256]{1,0:T(8,128)} %p.1), custom_call_target="tpu_custom_call" | custom-call | tf_op jit(solution)/shard_map/pallas_call | solution.py:587
  120.7 25.0 %shard_map.68 = (f32[256,256]{1,0:T(8,128)}, f32[256,256]{1,0:T(8,128)}, f32[256,256]{1,0:T(8,128)}) custom-call(f32[256,256]{1,0:T(8,128)} %get-tuple-element.6.a, f32[256,256]{1,0:T(8,128)} %get-tuple-element.7.b, f32[256,256]{1,0:T(8,128)} %get-tuple-element.8.c), custom_call_target="tpu_custom_call" | custom-call | tf_op jit(solution)/shard_map/pallas_call | solution.py:588

commit v3 on v0

v3 whole, which is shorter than its diff:
```python
import jax
import jax.numpy as jnp
from jax import lax
from jax.experimental import pallas as pl
from jax.experimental.pallas import tpu as pltpu
from jax.sharding import PartitionSpec as P

MESH = pl.DeviceIdType.MESH
F32 = jnp.float32
BF16 = jnp.bfloat16
F = 16
N = 256
H = 128
Z = 8
R4 = 4
R_X_FIRST, C_X_FIRST = (True, False), (True, False)
L_X_FIRST, Y_X_FIRST = (False, False), (True, True)


def split(v):
    hi = v.astype(BF16)
    return hi, (v - hi.astype(F32)).astype(BF16)


def dot3(a_hi, a_lo, b):
    b_hi, b_lo = split(b)
    out = jnp.dot(a_hi, b_hi, preferred_element_type=F32)
    out += jnp.dot(a_hi, b_lo, preferred_element_type=F32)
    return out + jnp.dot(a_lo, b_hi, preferred_element_type=F32)


def up(v, by, n):
    return lax.rem(v + by, n)


def arrived(ref, sem):
    pltpu.make_async_copy(ref, ref, sem).wait()


class Cond:
    def __init__(self, cond):
        self.cond = cond

    def __call__(self, body):
        pl.when(self.cond)(body)


class Task:
    def __init__(self, run, when=None):
        self.run, self.when = run, when


def run_all(*tasks):
    at = 0
    while at < len(tasks):
        when, end = tasks[at].when, at
        while end < len(tasks) and tasks[end].when is when:
            end += 1

        def group(part=tasks[at:end]):
            for one in part:
                one.run()

        if when is None:
            group()
        else:
            when(group)
        at = end


class Sends:
    def __init__(self, sem):
        self.sem, self.count, self.open = sem, 0, []

    def go(self, src, dst, recv, dev, kind, when=None):
        pltpu.make_async_remote_copy(
            src_ref=src, dst_ref=dst, send_sem=self.sem.at[self.count], recv_sem=recv, device_id=dev, device_id_type=MESH
        ).start()
        self.open.append((self.count, kind, when))
        self.count += 1

    def drain(self):
        for when in dict.fromkeys(w for _, _, w in self.open):
            def body(when=when):
                for n, kind, w in self.open:
                    if w is when:
                        arrived(kind, self.sem.at[n])
            if when is None:
                body()
            else:
                when(body)


class Ring4:
    def __init__(self, sends, ref, half, pos, plus, minus, sems, kind, kind_half, got, when=None, before=None):
        self.__dict__.update(locals())
        self.places = (pos, up(pos, 3, R4), up(pos, 1, R4), up(pos, 2, R4))
        self.start, self.end = Task(self.first, when), Task(self.last, when)
        self.mid0, self.mid1 = Task(lambda: self.pass_on(0), when), Task(lambda: self.pass_on(1), when)

    def first(self):
        if self.before:
            self.before()
        ref = self.ref(self.pos)
        self.sends.go(ref, ref, self.sems.at[0], self.plus, self.kind, self.when)
        self.sends.go(ref, ref, self.sems.at[1], self.minus, self.kind, self.when)
        self.got(self.pos, 0)

    def pass_on(self, side):
        at = self.places[1 + side]
        arrived(self.ref(at), self.sems.at[side])
        ref = self.half(at, side)
        self.sends.go(ref, ref, self.sems.at[2 + side], (self.plus, self.minus)[side], self.kind_half, self.when)
        self.got(at, 1 + side)

    def last(self):
        at = self.places[3]
        arrived(self.half(at, 0), self.sems.at[2])
        arrived(self.half(at, 1), self.sems.at[3])
        self.got(at, 3)


def kernel(
    st, r, l, p, root, cross, child,
    rg, rc, ro, lsame, lother, ysame, yother, oth_r, oth_l, oth_y, yown, lown, pg, jt_r, jt_l, jt_y, troot, tchild, rsr, rsc,
    s_send,
    s_rx, s_rp, s_rs, s_cx, s_cp, s_cs,
    s_rox, s_roy, s_ros, s_roo,
    s_lx, s_lox, s_ly, s_lp, s_ls, s_lo,
    s_yx, s_yox, s_yy, s_yp, s_ys, s_yo,
    s_p, s_pw, s_zr, s_zc,
):
    row, col = lax.axis_index("prow"), lax.axis_index("pcol")
    z, yh = lax.div(row, 2), lax.rem(row, 2)
    x, yl, core = lax.div(col, 4), lax.rem(lax.div(col, 2), 2), lax.rem(col, 2)
    y = 2 * yh + yl
    yn = 1 - yl

    def dev(zz, yy, xx, cc):
        return (2 * zz + lax.div(yy, 2), 4 * xx + 2 * lax.rem(yy, 2) + cc)

    xp, xm = dev(z, y, up(x, 1, 4), core), dev(z, y, up(x, 3, 4), core)
    zp, zm = dev(up(z, 1, Z), y, x, core), dev(up(z, 7, Z), y, x, core)
    sib = dev(z, y, x, 1 - core)
    yo = dev(z, up(y, 2, 4), x, core)
    pair = dev(z, 2 * yh + yn, x, core)
    cross_y = dev(z, 2 * (1 - yh) + yn, x, core)

    barrier = pltpu.get_barrier_semaphore()
    for d in (xp, xm, pair, cross_y, zp, zm, sib, yo):
        pl.semaphore_signal(barrier, inc=1, device_id=d, device_id_type=MESH)

    inside = Cond(core == yh)
    outside = Cond(core != yh)
    sends = Sends(s_send)
    v0 = 2 * x + yl
    for h in range(2):
        rg[pl.ds(2 * col + h, 1)] = r[:, H * h : H * h + H].reshape(1, N, H)
        lown[h] = l[:, H * h : H * h + H]
    pg[pl.ds(row, 1)] = p[...].reshape(1, H, N)

    @inside
    def _():
        for h in range(2):
            lsame[pl.ds(v0, 1), h] = l[:, H * h : H * h + H].reshape(1, N, H)

    pl.semaphore_wait(barrier, 8)

    k_2, k_1, k_h = rg.at[pl.ds(0, 2)], rg.at[0], rg.at[0, pl.ds(0, H)]

    class Group:
        pass

    def row_gather(buf, s_x, s_pair, s_sib, x_first):
        g = Group()
        g.ring, g.pair, g.passed = [None, None], [None, None], [[], []]

        def slot(at, yy, h):
            return 8 * at + 4 * yy + 2 * core + h

        def got(at, yy, h, k, pairing):
            ref = buf.at[slot(at, yy, h)]
            if pairing:
                sends.go(ref, ref, s_pair.at[h, k], pair, k_1)
            sends.go(ref, ref, s_sib.at[at, yy, h], sib, k_1)

        def lane(n, yy, h, before=None):
            return Ring4(
                sends, lambda at: buf.at[slot(at, yy, h)], lambda at, q: buf.at[slot(at, yy, h), pl.ds(H * q, H)],
                x, xp, xm, s_x.at[n], k_1, k_h, lambda at, k: got(at, yy, h, k, x_first[h]), None, before,
            )

        def own():
            for h in range(2):
                if not x_first[h]:
                    ref = buf.at[slot(x, yl, h)]
                    sends.go(ref, ref, s_pair.at[h, 0], pair, k_1)

        g.own = Task(own)
        for h in range(2):
            g.ring[h] = lane(h, yl, h)
            if x_first[h]:
                for k in range(4):
                    def passed(h=h, k=k, at=g.ring[h].places[k]):
                        arrived(k_1, s_pair.at[h, k])
                        got(at, yn, h, k, False)

                    g.passed[h].append(Task(passed))
            else:
                g.pair[h] = lane(2 + h, yn, h, lambda h=h: arrived(k_1, s_pair.at[h, 0]))

        def finish():
            for n in range(16):
                arrived(k_1, s_sib.at[n // 4, n // 2 % 2, n % 2])

        g.finish = Task(finish)
        return g

    def plane_gather(own, same, other, oth, s_x, s_ox, s_y, s_pair, s_sib, s_oth, x_first):
        g = Group()
        g.ring, g.pair, g.passed, g.own = [None, None], [None, None], [[], []], [None, None]
        g.out, g.outer, g.finish = [], [], []

        def got(buf, which, v, c, k, pairing):
            ref = buf.at[v, c]
            if pairing:
                sends.go(ref, ref, s_pair.at[c, k], pair, k_1, inside)
            sends.go(ref, ref, s_sib.at[which, c, v], sib, k_1, inside)

        def lane(buf, which, yy, c, sems, pairing, before=None):
            return Ring4(
                sends, lambda at: buf.at[2 * at + yy, c], lambda at, q: buf.at[2 * at + yy, c, pl.ds(H * q, H)],
                x, xp, xm, sems, k_1, k_h,
                lambda at, k: got(buf, which, 2 * at + yy, c, k, pairing), inside, before,
            )

        def from_other():
            oth[...] = other[pl.ds(v0, 1)].reshape(2, N, H)

        g.push_own = Task(lambda: sends.go(own, oth, s_oth.at[0], yo, k_2, inside), inside)
        g.take_own = Task(lambda: arrived(k_2, s_oth.at[0]), outside)
        g.copy_own = Task(from_other, inside)
        for c in range(2):
            if x_first and x_first[c]:
                g.ring[c] = lane(same, 0, yl, c, s_x.at[c], True)
                for k in range(4):
                    def passed(c=c, k=k, at=g.ring[c].places[k]):
                        arrived(k_1, s_pair.at[c, k])
                        got(same, 0, 2 * at + yn, c, k, False)

                    g.passed[c].append(Task(passed, inside))
            elif x_first:
                def push(c=c):
                    ref = same.at[v0, c]
                    sends.go(ref, ref, s_pair.at[c, 0], pair, k_1, inside)

                g.own[c] = Task(push, inside)
                g.ring[c] = lane(same, 0, yl, c, s_x.at[c], False)
                g.pair[c] = lane(same, 0, yn, c, s_x.at[2 + c], False, lambda c=c: arrived(k_1, s_pair.at[c, 0]))

            def out(c=c):
                sends.go(own.at[c], other.at[v0, c], s_y.at[c, 0], yo, k_1, outside)
                sends.go(own.at[c], other.at[v0, c], s_y.at[c, 1], cross_y, k_1, outside)

            def finish(c=c):
                for v in range(8):
                    if x_first:
                        arrived(k_1, s_sib.at[0, c, v])
                    arrived(k_1, s_sib.at[1, c, v])

            g.out.append(Task(out, outside))
            g.outer.append([
                lane(other, 1, yy, c, s_ox.at[c, q], False, lambda c=c, q=q: arrived(k_1, s_y.at[c, q]))
                for q, yy in enumerate((yl, yn))
            ])
            g.finish.append(Task(finish, outside))
        return g

    rr = row_gather(rg, s_rx, s_rp, s_rs, R_X_FIRST)
    cc = row_gather(rc, s_cx, s_cp, s_cs, C_X_FIRST)
    r_own = rg.at[pl.ds(2 * col, 2)]
    ra = plane_gather(r_own, None, ro, oth_r, None, s_rox, s_roy, None, s_ros, s_roo, None)
    la = plane_gather(lown, lsame, lother, oth_l, s_lx, s_lox, s_ly, s_lp, s_ls, s_lo, L_X_FIRST)
    ya = plane_gather(yown, ysame, yother, oth_y, s_yx, s_yox, s_yy, s_yp, s_ys, s_yo, Y_X_FIRST)

    def p_slot(lane, zz):
        return 2 * zz + (yh if lane == 0 else 1 - yh)

    def p_task(lane, side, step):
        n = p_slot(lane, up(z, Z - step if side == 0 else step, Z))

        def run():
            if step:
                arrived(pg.at[n], s_p.at[lane, side, step - 1])
            elif lane and not swapped:
                swapped.append(True)
                arrived(pg.at[n], s_pw.at[0])
            if step < 3:
                ref, kind = pg.at[n], pg.at[0]
            else:
                ref, kind = pg.at[n, pl.ds(64 * side, 64)], pg.at[0, pl.ds(0, 64)]
            sends.go(ref, ref, s_p.at[lane, side, step], zp if side == 0 else zm, kind)

        return Task(run)

    swapped = []
    panel = Group()
    panel.swap = Task(lambda: sends.go(pg.at[row], pg.at[row], s_pw.at[0], yo, pg.at[0]))
    panel.go = [[[p_task(lane, side, step) for step in range(4)] for side in range(2)] for lane in range(2)]

    def p_finish():
        for lane in range(2):
            n = p_slot(lane, up(z, 4, Z))
            for side in range(2):
                arrived(pg.at[n, pl.ds(64 * side, 64)], s_p.at[lane, side, 3])

    panel.finish = Task(p_finish)

    def zsum(t, slots, sems, last):
        g = Group()
        g.step, g.last = [[[None] * 2 for n in range(4)] for side in range(2)], []
        for c in range(2):
            for side in range(2):
                for n in range(4):
                    if n == 0 and side != c:
                        continue

                    def step(c=c, side=side, n=n):
                        d = up(z, 4 - n if side == 0 else 4 + n, Z)
                        if n > 1 or (n == 1 and side == c):
                            got = slots.at[side, n - 1, c]
                            arrived(got, sems.at[side, n - 1, c])
                            t[pl.ds(d, 1), c] += got[...].reshape(1, N, H)
                        sends.go(
                            t.at[d, c], slots.at[side, n, c], sems.at[side, n, c], zp if side == 0 else zm,
                            slots.at[0, 0, 0],
                        )

                    g.step[side][n][c] = Task(step)

            def done(c=c):
                arrived(slots.at[0, 3, c], sems.at[0, 3, c])
                arrived(slots.at[1, 3, c], sems.at[1, 3, c])
                last(c, (t[pl.ds(z, 1), c].reshape(N, H) + slots[0, 3, c] + slots[1, 3, c]).T)

            g.last.append(Task(done))
        return g

    def root_last(c, v):
        root[H * c : H * c + H, :] = v
        for h in range(2):
            rc[pl.ds(2 * col + h, 1), H * c : H * c + H] = v[:, H * h : H * h + H].reshape(1, H, H)

    def child_last(c, v):
        child[H * c : H * c + H, :] = v

    zr = zsum(troot, rsr, s_zr, root_last)
    zc = zsum(tchild, rsc, s_zc, child_last)

    def left(dst, same, oth):
        def run():
            for u, blk in enumerate((same, oth)):
                for h in range(2):
                    hi, lo = split(blk(h).T)
                    dst[0, H * h : H * h + H, N * u : N * u + N] = hi
                    dst[1, H * h : H * h + H, N * u : N * u + N] = lo

        return Task(run)

    left_r = left(jt_r, lambda h: rg[pl.ds(2 * col + h, 1)].reshape(N, H), lambda h: oth_r[h])
    left_l = left(jt_l, lambda h: lown[h], lambda h: oth_l[h])
    left_y = left(jt_y, lambda h: yown[h], lambda h: oth_y[h])

    def terms(t, jt, same, oth, add):
        made = [[None] * 2 for m in range(4)]
        for m in range(4):
            for c in range(2):
                def run(m=m, c=c):
                    d = (up(z, 4 + m, Z), up(z, 4 - m if m else 0, Z))
                    cols = [jnp.concatenate([same(e, c), oth[pl.ds(e, 1), c].reshape(N, H)], axis=0) for e in d]
                    out = dot3(jt[0], jt[1], jnp.concatenate(cols, axis=1))
                    for n, e in enumerate(d):
                        new = out[:, H * n : H * n + H].reshape(1, N, H)
                        t[pl.ds(e, 1), c] = t[pl.ds(e, 1), c] + new if add else new

                made[m][c] = Task(run)
        return made

    term_r = terms(troot, jt_r, lambda e, c: rg[pl.ds(4 * e + 2 * yh + c, 1)].reshape(N, H), ro, False)
    term_l = terms(tchild, jt_l, lambda e, c: lsame[pl.ds(e, 1), c].reshape(N, H), lother, False)
    term_y = terms(tchild, jt_y, lambda e, c: ysame[pl.ds(e, 1), c].reshape(N, H), yother, True)

    def panel_product(buf):
        def body(f, acc):
            lhs = jnp.concatenate([buf[st[2 * f]], buf[st[2 * f + 1]]], axis=1)
            hi, lo = split(lhs)
            return acc + dot3(hi, lo, pg[pl.ds(2 * f, 2)].reshape(N, N))

        return lax.fori_loop(0, F // 2, body, jnp.zeros((N, N), F32))

    def y_run():
        new = panel_product(rg)
        for h in range(2):
            yown[h] = new[:, H * h : H * h + H]

        @inside
        def _():
            for h in range(2):
                ysame[pl.ds(v0, 1), h] = yown[h].reshape(1, N, H)

    def cross_run():
        acc = panel_product(rc)
        for h in range(2):
            live = jnp.int32(0)
            for f in range(F):
                live += (st[f] == 2 * row + h).astype(jnp.int32)
            cross[H * h : H * h + H, :] = acc[H * h : H * h + H, :] * (-live.astype(F32))

    make_y, make_cross = Task(y_run), Task(cross_run)

    run_all(
        panel.swap, rr.own, rr.ring[0].start, panel.go[0][0][0], panel.go[0][1][0], rr.ring[1].start, ra.out[1],
        ra.out[0], rr.ring[0].mid1, panel.go[1][0][0], panel.go[1][1][0], panel.go[0][0][1], panel.go[0][1][1],
        rr.ring[0].mid0, rr.ring[1].mid1, rr.ring[1].mid0, rr.pair[1].start, ra.outer[1][1].start, panel.go[1][0][1],
        rr.ring[0].end, panel.go[1][1][1], ra.outer[1][0].start, rr.ring[1].end, ra.outer[0][1].start, la.own[0],
        la.ring[0].start, panel.go[0][1][2], la.out[1], panel.go[0][0][2], rr.pair[1].mid1, rr.pair[1].mid0, la.out[0],
        panel.go[1][1][2], ra.outer[0][0].start, panel.go[1][0][2], ra.outer[0][1].mid0, ra.push_own, panel.go[0][1][3],
        la.own[1], ra.copy_own, ra.outer[1][0].mid1, la.push_own, rr.passed[0][2], ra.outer[0][1].mid1,
        ra.outer[1][0].mid0, panel.go[0][0][3], panel.go[1][0][3], panel.go[1][1][3], la.ring[1].start,
        ra.outer[1][1].mid0, ra.outer[1][1].mid1, ra.outer[0][0].mid1, ra.outer[0][0].mid0, rr.passed[0][1],
        rr.pair[1].end, rr.passed[0][0], rr.passed[0][3], la.pair[0].start, panel.finish, rr.finish, ra.outer[1][0].end,
        la.outer[1][1].start, la.outer[1][0].start, make_y, ya.ring[1].start, ra.finish[1], ya.ring[0].start,
        ra.take_own, ra.outer[0][1].end, la.ring[1].mid0, left_r, ra.outer[1][1].end, la.outer[0][0].start,
        la.ring[0].mid1, ra.outer[0][0].end, term_r[0][1], ya.out[0], zr.step[1][0][1], la.outer[0][1].start,
        la.pair[0].mid0, la.outer[1][1].mid0, la.copy_own, la.pair[1].start, ra.finish[0], ya.push_own, term_r[0][0],
        zr.step[0][0][0], term_r[1][1], term_r[1][0], la.pair[0].mid1, zr.step[1][1][0], ya.ring[1].mid1,
        la.outer[1][0].mid1, la.ring[1].mid1, term_r[2][1], la.outer[1][1].mid1, ya.out[1], zr.step[0][1][1],
        ya.ring[1].mid0, zr.step[0][1][0], la.ring[0].mid0, zr.step[1][1][1], term_r[2][0], la.take_own,
        ya.ring[0].mid1, la.outer[0][0].mid1, ya.ring[0].mid0, zr.step[1][2][0], la.outer[1][0].mid0, zr.step[0][2][1],
        left_l, la.pair[1].mid1, ya.outer[0][1].start, ya.passed[1][0], ya.take_own, ya.outer[0][0].start,
        la.pair[1].mid0, term_r[3][1], zr.step[1][2][1], term_r[3][0], ya.passed[0][0], la.pair[0].end,
        ya.outer[1][1].start, zr.step[0][2][0], ya.ring[1].end, la.outer[1][0].end, ya.ring[0].end, la.outer[1][1].end,
        ya.outer[1][0].start, la.ring[0].end, ya.passed[1][1], ya.copy_own, la.ring[1].end, la.outer[0][1].mid0,
        la.outer[0][1].mid1, la.outer[0][0].mid0, left_y, ya.outer[0][1].mid0, zr.step[1][3][0], ya.outer[0][1].mid1,
        zr.step[0][3][1], la.finish[1], la.pair[1].end, zr.step[1][3][1], ya.outer[0][0].mid1, zr.step[0][3][0],
        ya.outer[0][0].mid0, ya.outer[1][1].mid0, term_l[2][1], ya.passed[1][2], ya.passed[0][1], term_l[1][1],
        term_l[0][1], ya.outer[1][1].mid1, ya.outer[1][0].mid0, term_l[3][1], ya.outer[1][0].mid1, la.outer[0][0].end,
        la.outer[0][1].end, ya.passed[0][2], la.finish[0], ya.passed[0][3], term_l[1][0], ya.outer[0][1].end,
        term_l[0][0], ya.outer[0][0].end, ya.finish[0], term_y[0][0], zc.step[0][0][0], ya.passed[1][3], zr.last[1],
        zr.last[0], ya.outer[1][1].end, cc.own, ya.outer[1][0].end, cc.ring[1].start, ya.finish[1], term_y[0][1],
        zc.step[1][0][1], cc.ring[0].start, term_y[1][1], term_y[1][0], term_y[2][1], zc.step[1][1][0],
        zc.step[0][1][0], cc.pair[1].start, zc.step[1][1][1], zc.step[0][1][1], term_l[2][0], term_l[3][0],
        term_y[2][0], cc.ring[0].mid1, zc.step[1][2][0], cc.passed[0][0], cc.ring[0].mid0, zc.step[0][2][0],
        cc.pair[1].mid1, zc.step[0][2][1], cc.pair[1].mid0, zc.step[1][2][1], term_y[3][0], cc.ring[1].mid0,
        cc.ring[0].end, cc.ring[1].mid1, zc.step[0][3][0], zc.step[1][3][0], cc.passed[0][1], term_y[3][1],
        zc.step[1][3][1], cc.ring[1].end, zc.step[0][3][1], cc.pair[1].end, cc.passed[0][2], cc.passed[0][3], cc.finish,
        zc.last[0], make_cross, zc.last[1],
    )
    sends.drain()


def finish(a, b, c, ao, bo, co):
    ao[...] = a[...]
    bo[...] = b[...]
    co[...] = c[...]


def shards(root_inv, child_inv, child_panel, structure):
    vmem = pl.BlockSpec(memory_space=pltpu.VMEM)
    dma = pltpu.SemaphoreType.DMA
    out = jax.ShapeDtypeStruct((N, N), F32)
    half = (2, N, H)
    plane = [dma((4, 4)), dma((2, 2, 4)), dma((2, 2)), dma((2, 4)), dma((2, 2, 8)), dma((1,))]
    line = [dma((4, 4)), dma((2, 4)), dma((4, 2, 2))]
    call = pl.pallas_call(
        kernel,
        out_shape=(out, out, out),
        in_specs=[pl.BlockSpec(memory_space=pltpu.SMEM), vmem, vmem, vmem],
        out_specs=(vmem, vmem, vmem),
        scratch_shapes=[
            pltpu.VMEM((32, N, H), F32),
            pltpu.VMEM((32, N, H), F32),
            pltpu.VMEM((Z,) + half, F32),
            pltpu.VMEM((Z,) + half, F32),
            pltpu.VMEM((Z,) + half, F32),
            pltpu.VMEM((Z,) + half, F32),
            pltpu.VMEM((Z,) + half, F32),
            pltpu.VMEM(half, F32),
            pltpu.VMEM(half, F32),
            pltpu.VMEM(half, F32),
            pltpu.VMEM(half, F32),
            pltpu.VMEM(half, F32),
            pltpu.VMEM((F, H, N), F32),
            pltpu.VMEM((2, N, 2 * N), BF16),
            pltpu.VMEM((2, N, 2 * N), BF16),
            pltpu.VMEM((2, N, 2 * N), BF16),
            pltpu.VMEM((Z,) + half, F32),
            pltpu.VMEM((Z,) + half, F32),
            pltpu.VMEM((2, 4) + half, F32),
            pltpu.VMEM((2, 4) + half, F32),
            dma((320,)),
            *line,
            *line,
            dma((2, 2, 4)), dma((2, 2)), dma((2, 2, 8)), dma((1,)),
            *plane,
            *plane,
            dma((2, 2, 4)), dma((1,)),
            dma((2, 4, 2)), dma((2, 4, 2)),
        ],
        compiler_params=pltpu.CompilerParams(
            collective_id=0, has_side_effects=True, vmem_limit_bytes=56 * 2**20
        ),
    )
    parts = call(structure, root_inv, child_inv, child_panel)
    return pl.pallas_call(
        finish, out_shape=(out, out, out), in_specs=[vmem] * 3, out_specs=(vmem, vmem, vmem)
    )(*parts)


def solution(mesh):
    placed = (P("prow", "pcol"), P("prow", "pcol"), P("prow", "pcol"), P())
    return jax.shard_map(
        shards,
        mesh=mesh,
        in_specs=placed,
        out_specs=(P("prow", "pcol"), P("prow", "pcol"), P("prow", "pcol")),
        check_vma=False,
    )
```

time: 925 us -> 100 us (0.11)
  waiting for transfers between devices: 855 us -> 0 us
  Pallas kernels: 0 us -> 99.5 us
  matrix products: 44.8 us -> 0 us
  between operations: 14.2 us -> 0.64 us
    reduce_scatter x3 -> x0, waiting for transfers between devices: 622 us -> none  [the longest x1 214 us: shards(): lax.psum_scatter(update_terms, 'prow', scatter_dimension=0, tiled=True)]
    all_gather x5 -> x0, waiting for transfers between devices: 231 us -> none  [the longest x1 86.5 us: shards(): gathered_rows = lax.all_gather(child_panel, 'prow', axis=0, tiled=True)]
    pallas_call x0 -> x2, Pallas kernels: none -> 99.5 us  [the longest x1 97.5 us: shards(): parts = call(structure, root_inv, child_inv, child_panel)]
    dot_general x5 -> x0, matrix products: 44.8 us -> none  [product(): jnp.einsum(subscripts, former, latter, precision=lax.Precision.HIGHEST, p...]
  transfers between devices with their start and end apart: 8 -> 0, of which waited for: 8 -> 0; matrix products, arithmetic and copies ran while one was open for 4% -> 0% of each run, Pallas kernels for 0% -> 0%
where the time goes in v3:
time: 100 us
  Pallas kernels  99.5 us (100%)
    pallas_call x1, Pallas kernels, shards(): parts = call(structure, root_inv, child_inv, child_panel)  97.5 us
    pallas_call x1, Pallas kernels, shards(): pl.pallas_call(finish, out_shape=(out, out, out), in_specs=[vmem] * 3, ou...  2 us

profile of v3, /device:TPU:1, one launch (start us, length us, event | category | flops | bytes accessed | tf_op | source)
XLA Modules:
  0.0 100.1 jit_solution(3194099714882657501)
XLA Ops:
  0.6 97.5 %shard_map.67 = (f32[256,256]{1,0:T(8,128)}, f32[256,256]{1,0:T(8,128)}, f32[256,256]{1,0:T(8,128)}) custom-call(s32[16]{0:T(128)} %st.1, f32[256,256]{1,0:T(8,128)} %r.1, f32[256,256]{1,0:T(8,128)} %l.1, f32[128,256]{1,0:T(8,128)} %p.1), custom_call_target="tpu_custom_call" | custom-call | tf_op jit(solution)/shard_map/pallas_call | solution.py:514
  98.1 2.0 %shard_map.68 = (f32[256,256]{1,0:T(8,128)}, f32[256,256]{1,0:T(8,128)}, f32[256,256]{1,0:T(8,128)}) custom-call(f32[256,256]{1,0:T(8,128)} %get-tuple-element.6.a, f32[256,256]{1,0:T(8,128)} %get-tuple-element.7.b, f32[256,256]{1,0:T(8,128)} %get-tuple-element.8.c), custom_call_target="tpu_custom_call" | custom-call | tf_op jit(solution)/shard_map/pallas_call | solution.py:515

commit v4 on v3

--- a/solution.py
+++ b/solution.py
@@ -1,3 +1,5 @@
+import math
+
 import jax
 import jax.numpy as jnp
 from jax import lax
@@ -11,7 +13,10 @@
 F = 16
 N = 256
 H = 128
+QUARTER = N // 4
 Z = 8
+GRID = 1
+PIECES = 2
 R4 = 4
 R_X_FIRST, C_X_FIRST = (True, False), (True, False)
 L_X_FIRST, Y_X_FIRST = (False, False), (True, True)
@@ -69,26 +74,40 @@
 
 
 class Sends:
-    def __init__(self, sem):
-        self.sem, self.count, self.open = sem, 0, []
+    def __init__(self, sem, whole):
+        self.sem, self.whole, self.open, self.sets = sem, whole, {}, []
 
     def go(self, src, dst, recv, dev, kind, when=None):
+        size = math.prod(kind.shape) // (H * QUARTER)
+        if (when, size == 1) not in self.open:
+            self.open[when, size == 1] = [len(self.sets), 0]
+            self.sets.append((when, self.open[when, size == 1]))
+        held = self.open[when, size == 1]
         pltpu.make_async_remote_copy(
-            src_ref=src, dst_ref=dst, send_sem=self.sem.at[self.count], recv_sem=recv, device_id=dev, device_id_type=MESH
+            src_ref=src, dst_ref=dst, send_sem=self.sem.at[held[0]], recv_sem=recv, device_id=dev, device_id_type=MESH
         ).start()
-        self.open.append((self.count, kind, when))
-        self.count += 1
+        held[1] += size
+        if held[1] >= 100 and held[1] % 4 == 0:
+            del self.open[when, size == 1]
 
     def drain(self):
-        for when in dict.fromkeys(w for _, _, w in self.open):
+        for when in dict.fromkeys(w for w, _ in self.sets):
             def body(when=when):
-                for n, kind, w in self.open:
+                for w, (n, quarters) in self.sets:
                     if w is when:
-                        arrived(kind, self.sem.at[n])
+                        arrived(self.bytes(quarters), self.sem.at[n])
+
             if when is None:
                 body()
             else:
                 when(body)
+
+    def bytes(self, quarters):
+        rows = QUARTER
+        while quarters % 2 == 0 and rows < N:
+            quarters, rows = quarters // 2, rows * 2
+        assert quarters <= self.whole.shape[0]
+        return self.whole.at[pl.ds(0, quarters), pl.ds(0, rows)]
 
 
 class Ring4:
@@ -152,7 +171,7 @@
 
     inside = Cond(core == yh)
     outside = Cond(core != yh)
-    sends = Sends(s_send)
+    sends = Sends(s_send, rg)
     v0 = 2 * x + yl
     for h in range(2):
         rg[pl.ds(2 * col + h, 1)] = r[:, H * h : H * h + H].reshape(1, N, H)
@@ -182,7 +201,7 @@
             ref = buf.at[slot(at, yy, h)]
             if pairing:
                 sends.go(ref, ref, s_pair.at[h, k], pair, k_1)
-            sends.go(ref, ref, s_sib.at[at, yy, h], sib, k_1)
+            sends.go(ref, ref, s_sib.at[0], sib, k_1)
 
         def lane(n, yy, h, before=None):
             return Ring4(
@@ -210,8 +229,7 @@
                 g.pair[h] = lane(2 + h, yn, h, lambda h=h: arrived(k_1, s_pair.at[h, 0]))
 
         def finish():
-            for n in range(16):
-                arrived(k_1, s_sib.at[n // 4, n // 2 % 2, n % 2])
+            arrived(buf.at[pl.ds(0, 16)], s_sib.at[0])
 
         g.finish = Task(finish)
         return g
@@ -225,7 +243,7 @@
             ref = buf.at[v, c]
             if pairing:
                 sends.go(ref, ref, s_pair.at[c, k], pair, k_1, inside)
-            sends.go(ref, ref, s_sib.at[which, c, v], sib, k_1, inside)
+            sends.go(ref, ref, s_sib.at[c], sib, k_1, inside)
 
         def lane(buf, which, yy, c, sems, pairing, before=None):
             return Ring4(
@@ -263,10 +281,7 @@
                 sends.go(own.at[c], other.at[v0, c], s_y.at[c, 1], cross_y, k_1, outside)
 
             def finish(c=c):
-                for v in range(8):
-                    if x_first:
-                        arrived(k_1, s_sib.at[0, c, v])
-                    arrived(k_1, s_sib.at[1, c, v])
+                arrived(rg.at[pl.ds(0, 16 if x_first else 8)], s_sib.at[c])
 
             g.out.append(Task(out, outside))
             g.outer.append([
@@ -286,61 +301,73 @@
     def p_slot(lane, zz):
         return 2 * zz + (yh if lane == 0 else 1 - yh)
 
-    def p_task(lane, side, step):
+    p_rows = H // PIECES
+
+    def p_ref(n, q):
+        return pg.at[n, pl.ds(p_rows * q, p_rows)]
+
+    def p_far(n, q, side):
+        return pg.at[n, pl.ds(p_rows * q + p_rows // 2 * side, p_rows // 2)]
+
+    def p_task(lane, q, side, step):
         n = p_slot(lane, up(z, Z - step if side == 0 else step, Z))
 
         def run():
             if step:
-                arrived(pg.at[n], s_p.at[lane, side, step - 1])
-            elif lane and not swapped:
-                swapped.append(True)
-                arrived(pg.at[n], s_pw.at[0])
-            if step < 3:
-                ref, kind = pg.at[n], pg.at[0]
-            else:
-                ref, kind = pg.at[n, pl.ds(64 * side, 64)], pg.at[0, pl.ds(0, 64)]
-            sends.go(ref, ref, s_p.at[lane, side, step], zp if side == 0 else zm, kind)
+                arrived(p_ref(n, q), s_p.at[lane, q, side, step - 1])
+            elif lane and q not in swapped:
+                swapped.append(q)
+                arrived(p_ref(n, q), s_pw.at[q])
+            ref, kind = (p_ref(n, q), p_ref(0, 0)) if step < 3 else (p_far(n, q, side), p_far(0, 0, 0))
+            sends.go(ref, ref, s_p.at[lane, q, side, step], zp if side == 0 else zm, kind)
 
         return Task(run)
+
+    def p_swap(q):
+        return Task(lambda: sends.go(p_ref(row, q), p_ref(row, q), s_pw.at[q], yo, p_ref(0, 0)))
 
     swapped = []
     panel = Group()
-    panel.swap = Task(lambda: sends.go(pg.at[row], pg.at[row], s_pw.at[0], yo, pg.at[0]))
-    panel.go = [[[p_task(lane, side, step) for step in range(4)] for side in range(2)] for lane in range(2)]
+    panel.swap = [p_swap(q) for q in range(PIECES)]
+    panel.go = [
+        [[[p_task(lane, q, side, step) for step in range(4)] for side in range(2)] for q in range(PIECES)]
+        for lane in range(2)
+    ]
 
     def p_finish():
         for lane in range(2):
             n = p_slot(lane, up(z, 4, Z))
-            for side in range(2):
-                arrived(pg.at[n, pl.ds(64 * side, 64)], s_p.at[lane, side, 3])
+            for q in range(PIECES):
+                for side in range(2):
+                    arrived(p_far(n, q, side), s_p.at[lane, q, side, 3])
 
     panel.finish = Task(p_finish)
 
     def zsum(t, slots, sems, last):
         g = Group()
-        g.step, g.last = [[[None] * 2 for n in range(4)] for side in range(2)], []
+        g.step, g.last = [[[[None] * PIECES for c in range(2)] for n in range(4)] for side in range(2)], []
+        rows = N // PIECES
         for c in range(2):
-            for side in range(2):
-                for n in range(4):
-                    if n == 0 and side != c:
-                        continue
-
-                    def step(c=c, side=side, n=n):
-                        d = up(z, 4 - n if side == 0 else 4 + n, Z)
-                        if n > 1 or (n == 1 and side == c):
-                            got = slots.at[side, n - 1, c]
-                            arrived(got, sems.at[side, n - 1, c])
-                            t[pl.ds(d, 1), c] += got[...].reshape(1, N, H)
-                        sends.go(
-                            t.at[d, c], slots.at[side, n, c], sems.at[side, n, c], zp if side == 0 else zm,
-                            slots.at[0, 0, 0],
-                        )
-
-                    g.step[side][n][c] = Task(step)
+            for q in range(PIECES):
+                for side in range(2):
+                    for n in range(1 if side != c else 0, 4):
+                        def step(c=c, q=q, side=side, n=n, run=pl.ds(rows * q, rows)):
+                            d = up(z, 4 - n if side == 0 else 4 + n, Z)
+                            if n > 1 or (n == 1 and side == c):
+                                got = slots.at[side, n - 1, c, run]
+                                arrived(got, sems.at[side, n - 1, c, q])
+                                t[pl.ds(d, 1), c, run] += got[...].reshape(1, rows, H)
+                            sends.go(
+                                t.at[d, c, run], slots.at[side, n, c, run], sems.at[side, n, c, q],
+                                zp if side == 0 else zm, slots.at[0, 0, 0, pl.ds(0, rows)],
+                            )
+
+                        g.step[side][n][c][q] = Task(step)
 
             def done(c=c):
-                arrived(slots.at[0, 3, c], sems.at[0, 3, c])
-                arrived(slots.at[1, 3, c], sems.at[1, 3, c])
+                for side in range(2):
+                    for q in range(PIECES):
+                        arrived(slots.at[side, 3, c, pl.ds(rows * q, rows)], sems.at[side, 3, c, q])
                 last(c, (t[pl.ds(z, 1), c].reshape(N, H) + slots[0, 3, c] + slots[1, 3, c]).T)
 
             g.last.append(Task(done))
@@ -419,42 +446,52 @@
     make_y, make_cross = Task(y_run), Task(cross_run)
 
     run_all(
-        panel.swap, rr.own, rr.ring[0].start, panel.go[0][0][0], panel.go[0][1][0], rr.ring[1].start, ra.out[1],
-        ra.out[0], rr.ring[0].mid1, panel.go[1][0][0], panel.go[1][1][0], panel.go[0][0][1], panel.go[0][1][1],
-        rr.ring[0].mid0, rr.ring[1].mid1, rr.ring[1].mid0, rr.pair[1].start, ra.outer[1][1].start, panel.go[1][0][1],
-        rr.ring[0].end, panel.go[1][1][1], ra.outer[1][0].start, rr.ring[1].end, ra.outer[0][1].start, la.own[0],
-        la.ring[0].start, panel.go[0][1][2], la.out[1], panel.go[0][0][2], rr.pair[1].mid1, rr.pair[1].mid0, la.out[0],
-        panel.go[1][1][2], ra.outer[0][0].start, panel.go[1][0][2], ra.outer[0][1].mid0, ra.push_own, panel.go[0][1][3],
-        la.own[1], ra.copy_own, ra.outer[1][0].mid1, la.push_own, rr.passed[0][2], ra.outer[0][1].mid1,
-        ra.outer[1][0].mid0, panel.go[0][0][3], panel.go[1][0][3], panel.go[1][1][3], la.ring[1].start,
-        ra.outer[1][1].mid0, ra.outer[1][1].mid1, ra.outer[0][0].mid1, ra.outer[0][0].mid0, rr.passed[0][1],
-        rr.pair[1].end, rr.passed[0][0], rr.passed[0][3], la.pair[0].start, panel.finish, rr.finish, ra.outer[1][0].end,
-        la.outer[1][1].start, la.outer[1][0].start, make_y, ya.ring[1].start, ra.finish[1], ya.ring[0].start,
-        ra.take_own, ra.outer[0][1].end, la.ring[1].mid0, left_r, ra.outer[1][1].end, la.outer[0][0].start,
-        la.ring[0].mid1, ra.outer[0][0].end, term_r[0][1], ya.out[0], zr.step[1][0][1], la.outer[0][1].start,
-        la.pair[0].mid0, la.outer[1][1].mid0, la.copy_own, la.pair[1].start, ra.finish[0], ya.push_own, term_r[0][0],
-        zr.step[0][0][0], term_r[1][1], term_r[1][0], la.pair[0].mid1, zr.step[1][1][0], ya.ring[1].mid1,
-        la.outer[1][0].mid1, la.ring[1].mid1, term_r[2][1], la.outer[1][1].mid1, ya.out[1], zr.step[0][1][1],
-        ya.ring[1].mid0, zr.step[0][1][0], la.ring[0].mid0, zr.step[1][1][1], term_r[2][0], la.take_own,
-        ya.ring[0].mid1, la.outer[0][0].mid1, ya.ring[0].mid0, zr.step[1][2][0], la.outer[1][0].mid0, zr.step[0][2][1],
-        left_l, la.pair[1].mid1, ya.outer[0][1].start, ya.passed[1][0], ya.take_own, ya.outer[0][0].start,
-        la.pair[1].mid0, term_r[3][1], zr.step[1][2][1], term_r[3][0], ya.passed[0][0], la.pair[0].end,
-        ya.outer[1][1].start, zr.step[0][2][0], ya.ring[1].end, la.outer[1][0].end, ya.ring[0].end, la.outer[1][1].end,
-        ya.outer[1][0].start, la.ring[0].end, ya.passed[1][1], ya.copy_own, la.ring[1].end, la.outer[0][1].mid0,
-        la.outer[0][1].mid1, la.outer[0][0].mid0, left_y, ya.outer[0][1].mid0, zr.step[1][3][0], ya.outer[0][1].mid1,
-        zr.step[0][3][1], la.finish[1], la.pair[1].end, zr.step[1][3][1], ya.outer[0][0].mid1, zr.step[0][3][0],
-        ya.outer[0][0].mid0, ya.outer[1][1].mid0, term_l[2][1], ya.passed[1][2], ya.passed[0][1], term_l[1][1],
-        term_l[0][1], ya.outer[1][1].mid1, ya.outer[1][0].mid0, term_l[3][1], ya.outer[1][0].mid1, la.outer[0][0].end,
-        la.outer[0][1].end, ya.passed[0][2], la.finish[0], ya.passed[0][3], term_l[1][0], ya.outer[0][1].end,
-        term_l[0][0], ya.outer[0][0].end, ya.finish[0], term_y[0][0], zc.step[0][0][0], ya.passed[1][3], zr.last[1],
-        zr.last[0], ya.outer[1][1].end, cc.own, ya.outer[1][0].end, cc.ring[1].start, ya.finish[1], term_y[0][1],
-        zc.step[1][0][1], cc.ring[0].start, term_y[1][1], term_y[1][0], term_y[2][1], zc.step[1][1][0],
-        zc.step[0][1][0], cc.pair[1].start, zc.step[1][1][1], zc.step[0][1][1], term_l[2][0], term_l[3][0],
-        term_y[2][0], cc.ring[0].mid1, zc.step[1][2][0], cc.passed[0][0], cc.ring[0].mid0, zc.step[0][2][0],
-        cc.pair[1].mid1, zc.step[0][2][1], cc.pair[1].mid0, zc.step[1][2][1], term_y[3][0], cc.ring[1].mid0,
-        cc.ring[0].end, cc.ring[1].mid1, zc.step[0][3][0], zc.step[1][3][0], cc.passed[0][1], term_y[3][1],
-        zc.step[1][3][1], cc.ring[1].end, zc.step[0][3][1], cc.pair[1].end, cc.passed[0][2], cc.passed[0][3], cc.finish,
-        zc.last[0], make_cross, zc.last[1],
+        rr.own, panel.swap[1], panel.swap[0], panel.go[0][0][1][0], panel.go[0][0][0][0], rr.ring[0].start, ra.out[0],
+        panel.go[0][1][0][0], rr.ring[1].start, ra.out[1], rr.pair[1].start, rr.ring[0].mid1, panel.go[0][0][0][1],
+        rr.ring[0].mid0, panel.go[0][1][1][0], panel.go[0][1][0][1], panel.go[0][0][1][1], rr.ring[1].mid1,
+        panel.go[1][1][1][0], rr.ring[1].mid0, panel.go[1][0][0][0], panel.go[1][0][1][0], panel.go[1][1][0][0],
+        ra.outer[0][1].start, ra.outer[1][1].start, ra.push_own, panel.go[0][1][1][1], rr.pair[1].mid1, rr.pair[1].mid0,
+        panel.go[0][0][0][2], rr.ring[0].end, panel.go[0][1][0][2], panel.go[1][1][1][1], rr.ring[1].end, la.own[0],
+        panel.go[1][0][1][1], ra.outer[0][0].start, la.own[1], panel.go[1][0][0][1], panel.go[1][1][0][1], la.out[0],
+        la.ring[0].start, ra.outer[0][1].mid1, panel.go[0][0][1][2], ra.outer[1][1].mid1, la.out[1],
+        panel.go[0][1][1][2], panel.go[1][1][1][2], rr.passed[0][2], ra.outer[1][0].start, ra.outer[0][1].mid0,
+        panel.go[0][1][0][3], panel.go[1][0][1][2], panel.go[1][0][0][2], ra.outer[0][0].mid0, ra.take_own,
+        ra.outer[1][1].mid0, panel.go[1][1][0][2], rr.passed[0][0], ra.copy_own, ra.outer[0][0].mid1, la.ring[0].mid0,
+        rr.pair[1].end, left_r, la.ring[0].mid1, la.outer[0][1].start, la.ring[1].start, rr.passed[0][3],
+        rr.passed[0][1], panel.go[0][0][1][3], ra.outer[1][0].mid1, panel.go[0][1][1][3], panel.go[1][1][1][3],
+        ra.outer[1][0].mid0, panel.go[0][0][0][3], panel.go[1][0][0][3], panel.go[1][0][1][3], ra.outer[0][1].end,
+        panel.go[1][1][0][3], ra.outer[0][0].end, la.outer[1][1].start, ra.finish[0], la.pair[0].start,
+        ra.outer[1][1].end, rr.finish, term_r[2][0], term_r[0][0], la.ring[0].end, term_r[1][0], zr.step[1][1][0][0],
+        zr.step[1][1][0][1], la.push_own, zr.step[0][0][0][1], zr.step[0][0][0][0], la.pair[1].start,
+        la.outer[0][1].mid0, la.outer[0][1].mid1, panel.finish, la.outer[0][0].start, make_y, ra.outer[1][0].end,
+        ya.ring[1].start, ya.out[0], ra.finish[1], term_r[0][1], ya.ring[0].start, zr.step[1][0][1][0],
+        zr.step[1][0][1][1], zr.step[0][1][0][1], term_r[3][0], term_r[1][1], zr.step[0][1][1][1], ya.out[1],
+        term_r[2][1], la.pair[1].mid0, la.pair[0].mid0, la.ring[1].mid1, zr.step[1][2][0][0], la.outer[1][0].start,
+        la.pair[0].mid1, la.ring[1].mid0, zr.step[0][1][0][0], zr.step[0][1][1][0], la.outer[0][0].mid0,
+        la.outer[1][1].mid1, zr.step[1][1][1][0], la.outer[1][1].mid0, la.outer[0][0].mid1, la.pair[1].mid1,
+        zr.step[1][1][1][1], term_r[3][1], ya.passed[0][0], zr.step[1][2][0][1], ya.ring[1].mid1, ya.ring[0].mid1,
+        ya.ring[1].mid0, ya.ring[0].mid0, la.outer[0][1].end, zr.step[0][2][0][1], ya.outer[0][1].start,
+        zr.step[1][3][0][0], zr.step[0][2][1][0], ya.outer[0][0].start, zr.step[0][2][0][0], zr.step[0][2][1][1],
+        la.outer[1][0].mid0, ya.push_own, zr.step[1][2][1][0], ya.outer[1][1].start, zr.step[1][2][1][1],
+        ya.outer[1][0].start, ya.ring[0].end, la.outer[1][1].end, la.outer[1][0].mid1, ya.outer[0][1].mid0,
+        la.outer[0][0].end, ya.outer[0][1].mid1, zr.step[0][3][0][1], zr.step[1][3][0][1], zr.step[0][3][0][0],
+        ya.outer[0][0].mid0, zr.step[0][3][1][0], ya.passed[0][2], ya.ring[1].end, zr.step[0][3][1][1], la.ring[1].end,
+        la.take_own, ya.outer[0][0].mid1, ya.take_own, la.pair[0].end, zr.step[1][3][1][0], zr.step[1][3][1][1],
+        la.copy_own, ya.copy_own, left_l, la.finish[0], term_l[3][0], term_l[0][0], ya.outer[1][1].mid0, term_l[1][0],
+        ya.passed[0][1], ya.outer[1][0].mid1, la.finish[1], term_l[2][0], ya.passed[1][0], la.pair[1].end, left_y,
+        la.outer[1][0].end, ya.finish[0], ya.outer[1][0].mid0, ya.passed[1][1], ya.passed[0][3], ya.outer[1][1].mid1,
+        ya.outer[0][0].end, ya.outer[0][1].end, term_y[1][0], zc.step[1][1][0][0], zc.step[1][1][0][1], term_y[0][0],
+        zc.step[0][0][0][1], zr.last[0], zc.step[0][0][0][0], zr.last[1], cc.own, cc.ring[0].start, ya.passed[1][3],
+        term_l[3][1], ya.passed[1][2], cc.ring[1].start, term_l[0][1], term_l[1][1], ya.outer[1][1].end, ya.finish[1],
+        ya.outer[1][0].end, term_y[0][1], zc.step[1][0][1][0], term_y[1][1], zc.step[1][0][1][1], zc.step[0][1][1][0],
+        zc.step[0][1][1][1], term_y[2][0], term_y[3][0], zc.step[1][2][0][0], zc.step[0][1][0][0], term_l[2][1],
+        zc.step[0][1][0][1], cc.pair[1].start, zc.step[1][2][0][1], cc.ring[0].mid1, cc.ring[0].mid0,
+        zc.step[1][1][1][0], term_y[3][1], cc.passed[0][0], cc.ring[1].mid0, zc.step[1][1][1][1], term_y[2][1],
+        zc.step[0][2][1][1], zc.step[0][2][1][0], cc.ring[1].mid1, zc.step[0][2][0][0], zc.step[1][3][0][0],
+        zc.step[0][2][0][1], cc.pair[1].mid1, zc.step[1][2][1][0], cc.pair[1].mid0, cc.ring[0].end, zc.step[1][2][1][1],
+        cc.ring[1].end, zc.step[0][3][1][1], zc.step[1][3][0][1], cc.passed[0][1], zc.step[0][3][0][0],
+        zc.step[0][3][0][1], zc.step[1][3][1][0], cc.pair[1].end, zc.step[0][3][1][0], cc.passed[0][2],
+        zc.step[1][3][1][1], cc.passed[0][3], cc.finish, make_cross, zc.last[0], zc.last[1],
     )
     sends.drain()
 
@@ -469,9 +506,10 @@
     vmem = pl.BlockSpec(memory_space=pltpu.VMEM)
     dma = pltpu.SemaphoreType.DMA
     out = jax.ShapeDtypeStruct((N, N), F32)
+    rows = pl.BlockSpec((N // GRID, N), lambda n: (n, 0))
     half = (2, N, H)
-    plane = [dma((4, 4)), dma((2, 2, 4)), dma((2, 2)), dma((2, 4)), dma((2, 2, 8)), dma((1,))]
-    line = [dma((4, 4)), dma((2, 4)), dma((4, 2, 2))]
+    plane = [dma((4, 4)), dma((2, 2, 4)), dma((2, 2)), dma((2, 4)), dma((2,)), dma((1,))]
+    line = [dma((4, 4)), dma((2, 4)), dma((1,))]
     call = pl.pallas_call(
         kernel,
         out_shape=(out, out, out),
@@ -498,14 +536,14 @@
             pltpu.VMEM((Z,) + half, F32),
             pltpu.VMEM((2, 4) + half, F32),
             pltpu.VMEM((2, 4) + half, F32),
-            dma((320,)),
+            dma((24,)),
             *line,
             *line,
-            dma((2, 2, 4)), dma((2, 2)), dma((2, 2, 8)), dma((1,)),
+            dma((2, 2, 4)), dma((2, 2)), dma((2,)), dma((1,)),
             *plane,
             *plane,
-            dma((2, 2, 4)), dma((1,)),
-            dma((2, 4, 2)), dma((2, 4, 2)),
+            dma((2, PIECES, 2, 4)), dma((PIECES,)),
+            dma((2, 4, 2, PIECES)), dma((2, 4, 2, PIECES)),
         ],
         compiler_params=pltpu.CompilerParams(
             collective_id=0, has_side_effects=True, vmem_limit_bytes=56 * 2**20
@@ -513,7 +551,7 @@
     )
     parts = call(structure, root_inv, child_inv, child_panel)
     return pl.pallas_call(
-        finish, out_shape=(out, out, out), in_specs=[vmem] * 3, out_specs=(vmem, vmem, vmem)
+        finish, grid=(GRID,), out_shape=(out, out, out), in_specs=[rows] * 3, out_specs=(rows, rows, rows)
     )(*parts)
 
 

time: 100 us -> 93.8 us (0.938)
  Pallas kernels: 99.5 us -> 93 us
    pallas_call x1, Pallas kernels: 97.5 us -> 91 us  [shards(): parts = call(structure, root_inv, child_inv, child_panel)]
where the time goes in v4:
time: 93.8 us; the launch traced here: 93.7 us
  Pallas kernels  93 us (99%)
    pallas_call x1, Pallas kernels, shards(): parts = call(structure, root_inv, child_inv, child_panel)  91 us
    pallas_call x1, Pallas kernels, shards(): pl.pallas_call(finish, grid=(GRID,), out_shape=(out, out, out), in_specs=...  2 us

profile of v4, /device:TPU:1, one launch (start us, length us, event | category | flops | bytes accessed | tf_op | source)
XLA Modules:
  0.0 93.7 jit_solution(4478683576507262999)
XLA Ops:
  0.6 91.0 %shard_map.67 = (f32[256,256]{1,0:T(8,128)}, f32[256,256]{1,0:T(8,128)}, f32[256,256]{1,0:T(8,128)}) custom-call(s32[16]{0:T(128)} %st.1, f32[256,256]{1,0:T(8,128)} %r.1, f32[256,256]{1,0:T(8,128)} %l.1, f32[128,256]{1,0:T(8,128)} %p.1), custom_call_target="tpu_custom_call" | custom-call | tf_op jit(solution)/shard_map/pallas_call | solution.py:552
  91.7 2.0 %shard_map.68 = (f32[256,256]{1,0:T(8,128)}, f32[256,256]{1,0:T(8,128)}, f32[256,256]{1,0:T(8,128)}) custom-call(f32[256,256]{1,0:T(8,128)} %get-tuple-element.6.a, f32[256,256]{1,0:T(8,128)} %get-tuple-element.7.b, f32[256,256]{1,0:T(8,128)} %get-tuple-element.8.c), custom_call_target="tpu_custom_call" | custom-call | tf_op jit(solution)/shard_map/pallas_call | solution.py:553

commit v5 on v4

--- a/solution.py
+++ b/solution.py
@@ -19,7 +19,7 @@
 PIECES = 2
 R4 = 4
 R_X_FIRST, C_X_FIRST = (True, False), (True, False)
-L_X_FIRST, Y_X_FIRST = (False, False), (True, True)
+L_X_FIRST, Y_X_FIRST = (True, False), (True, True)
 
 
 def split(v):
@@ -87,7 +87,7 @@
             src_ref=src, dst_ref=dst, send_sem=self.sem.at[held[0]], recv_sem=recv, device_id=dev, device_id_type=MESH
         ).start()
         held[1] += size
-        if held[1] >= 100 and held[1] % 4 == 0:
+        if held[1] >= 56 and held[1] % 4 == 0:
             del self.open[when, size == 1]
 
     def drain(self):
@@ -423,7 +423,7 @@
             hi, lo = split(lhs)
             return acc + dot3(hi, lo, pg[pl.ds(2 * f, 2)].reshape(N, N))
 
-        return lax.fori_loop(0, F // 2, body, jnp.zeros((N, N), F32))
+        return lax.fori_loop(0, F // 2, body, jnp.zeros((N, N), F32), unroll=True)
 
     def y_run():
         new = panel_product(rg)
@@ -446,52 +446,52 @@
     make_y, make_cross = Task(y_run), Task(cross_run)
 
     run_all(
-        rr.own, panel.swap[1], panel.swap[0], panel.go[0][0][1][0], panel.go[0][0][0][0], rr.ring[0].start, ra.out[0],
-        panel.go[0][1][0][0], rr.ring[1].start, ra.out[1], rr.pair[1].start, rr.ring[0].mid1, panel.go[0][0][0][1],
-        rr.ring[0].mid0, panel.go[0][1][1][0], panel.go[0][1][0][1], panel.go[0][0][1][1], rr.ring[1].mid1,
-        panel.go[1][1][1][0], rr.ring[1].mid0, panel.go[1][0][0][0], panel.go[1][0][1][0], panel.go[1][1][0][0],
-        ra.outer[0][1].start, ra.outer[1][1].start, ra.push_own, panel.go[0][1][1][1], rr.pair[1].mid1, rr.pair[1].mid0,
-        panel.go[0][0][0][2], rr.ring[0].end, panel.go[0][1][0][2], panel.go[1][1][1][1], rr.ring[1].end, la.own[0],
-        panel.go[1][0][1][1], ra.outer[0][0].start, la.own[1], panel.go[1][0][0][1], panel.go[1][1][0][1], la.out[0],
-        la.ring[0].start, ra.outer[0][1].mid1, panel.go[0][0][1][2], ra.outer[1][1].mid1, la.out[1],
-        panel.go[0][1][1][2], panel.go[1][1][1][2], rr.passed[0][2], ra.outer[1][0].start, ra.outer[0][1].mid0,
-        panel.go[0][1][0][3], panel.go[1][0][1][2], panel.go[1][0][0][2], ra.outer[0][0].mid0, ra.take_own,
-        ra.outer[1][1].mid0, panel.go[1][1][0][2], rr.passed[0][0], ra.copy_own, ra.outer[0][0].mid1, la.ring[0].mid0,
-        rr.pair[1].end, left_r, la.ring[0].mid1, la.outer[0][1].start, la.ring[1].start, rr.passed[0][3],
-        rr.passed[0][1], panel.go[0][0][1][3], ra.outer[1][0].mid1, panel.go[0][1][1][3], panel.go[1][1][1][3],
-        ra.outer[1][0].mid0, panel.go[0][0][0][3], panel.go[1][0][0][3], panel.go[1][0][1][3], ra.outer[0][1].end,
-        panel.go[1][1][0][3], ra.outer[0][0].end, la.outer[1][1].start, ra.finish[0], la.pair[0].start,
-        ra.outer[1][1].end, rr.finish, term_r[2][0], term_r[0][0], la.ring[0].end, term_r[1][0], zr.step[1][1][0][0],
-        zr.step[1][1][0][1], la.push_own, zr.step[0][0][0][1], zr.step[0][0][0][0], la.pair[1].start,
-        la.outer[0][1].mid0, la.outer[0][1].mid1, panel.finish, la.outer[0][0].start, make_y, ra.outer[1][0].end,
-        ya.ring[1].start, ya.out[0], ra.finish[1], term_r[0][1], ya.ring[0].start, zr.step[1][0][1][0],
-        zr.step[1][0][1][1], zr.step[0][1][0][1], term_r[3][0], term_r[1][1], zr.step[0][1][1][1], ya.out[1],
-        term_r[2][1], la.pair[1].mid0, la.pair[0].mid0, la.ring[1].mid1, zr.step[1][2][0][0], la.outer[1][0].start,
-        la.pair[0].mid1, la.ring[1].mid0, zr.step[0][1][0][0], zr.step[0][1][1][0], la.outer[0][0].mid0,
-        la.outer[1][1].mid1, zr.step[1][1][1][0], la.outer[1][1].mid0, la.outer[0][0].mid1, la.pair[1].mid1,
-        zr.step[1][1][1][1], term_r[3][1], ya.passed[0][0], zr.step[1][2][0][1], ya.ring[1].mid1, ya.ring[0].mid1,
-        ya.ring[1].mid0, ya.ring[0].mid0, la.outer[0][1].end, zr.step[0][2][0][1], ya.outer[0][1].start,
-        zr.step[1][3][0][0], zr.step[0][2][1][0], ya.outer[0][0].start, zr.step[0][2][0][0], zr.step[0][2][1][1],
-        la.outer[1][0].mid0, ya.push_own, zr.step[1][2][1][0], ya.outer[1][1].start, zr.step[1][2][1][1],
-        ya.outer[1][0].start, ya.ring[0].end, la.outer[1][1].end, la.outer[1][0].mid1, ya.outer[0][1].mid0,
-        la.outer[0][0].end, ya.outer[0][1].mid1, zr.step[0][3][0][1], zr.step[1][3][0][1], zr.step[0][3][0][0],
-        ya.outer[0][0].mid0, zr.step[0][3][1][0], ya.passed[0][2], ya.ring[1].end, zr.step[0][3][1][1], la.ring[1].end,
-        la.take_own, ya.outer[0][0].mid1, ya.take_own, la.pair[0].end, zr.step[1][3][1][0], zr.step[1][3][1][1],
-        la.copy_own, ya.copy_own, left_l, la.finish[0], term_l[3][0], term_l[0][0], ya.outer[1][1].mid0, term_l[1][0],
-        ya.passed[0][1], ya.outer[1][0].mid1, la.finish[1], term_l[2][0], ya.passed[1][0], la.pair[1].end, left_y,
-        la.outer[1][0].end, ya.finish[0], ya.outer[1][0].mid0, ya.passed[1][1], ya.passed[0][3], ya.outer[1][1].mid1,
-        ya.outer[0][0].end, ya.outer[0][1].end, term_y[1][0], zc.step[1][1][0][0], zc.step[1][1][0][1], term_y[0][0],
-        zc.step[0][0][0][1], zr.last[0], zc.step[0][0][0][0], zr.last[1], cc.own, cc.ring[0].start, ya.passed[1][3],
-        term_l[3][1], ya.passed[1][2], cc.ring[1].start, term_l[0][1], term_l[1][1], ya.outer[1][1].end, ya.finish[1],
-        ya.outer[1][0].end, term_y[0][1], zc.step[1][0][1][0], term_y[1][1], zc.step[1][0][1][1], zc.step[0][1][1][0],
-        zc.step[0][1][1][1], term_y[2][0], term_y[3][0], zc.step[1][2][0][0], zc.step[0][1][0][0], term_l[2][1],
-        zc.step[0][1][0][1], cc.pair[1].start, zc.step[1][2][0][1], cc.ring[0].mid1, cc.ring[0].mid0,
-        zc.step[1][1][1][0], term_y[3][1], cc.passed[0][0], cc.ring[1].mid0, zc.step[1][1][1][1], term_y[2][1],
-        zc.step[0][2][1][1], zc.step[0][2][1][0], cc.ring[1].mid1, zc.step[0][2][0][0], zc.step[1][3][0][0],
-        zc.step[0][2][0][1], cc.pair[1].mid1, zc.step[1][2][1][0], cc.pair[1].mid0, cc.ring[0].end, zc.step[1][2][1][1],
-        cc.ring[1].end, zc.step[0][3][1][1], zc.step[1][3][0][1], cc.passed[0][1], zc.step[0][3][0][0],
-        zc.step[0][3][0][1], zc.step[1][3][1][0], cc.pair[1].end, zc.step[0][3][1][0], cc.passed[0][2],
-        zc.step[1][3][1][1], cc.passed[0][3], cc.finish, make_cross, zc.last[0], zc.last[1],
+        panel.swap[1], panel.swap[0], panel.go[0][0][1][0], panel.go[0][0][0][0], rr.own, rr.ring[0].start,
+        rr.ring[1].start, panel.go[0][1][1][0], ra.out[0], ra.out[1], panel.go[0][1][0][0], panel.go[1][1][1][0],
+        panel.go[1][0][1][0], rr.ring[0].mid0, panel.go[1][1][0][0], panel.go[0][1][1][1], panel.go[0][0][0][1],
+        rr.ring[0].mid1, panel.go[0][0][1][1], rr.ring[1].mid1, rr.ring[1].mid0, rr.pair[1].start, panel.go[1][0][0][0],
+        rr.ring[0].end, panel.go[0][1][0][1], panel.go[1][1][0][1], panel.go[1][1][1][1], ra.outer[0][1].start,
+        ra.push_own, panel.go[1][0][1][1], ra.outer[1][1].start, panel.go[0][0][0][2], rr.pair[1].mid0, rr.ring[1].end,
+        la.own[1], panel.go[1][0][0][1], ra.outer[0][0].start, panel.go[0][0][1][2], ra.outer[1][0].start,
+        panel.go[1][1][1][2], la.out[1], la.ring[0].start, panel.go[0][1][1][2], panel.go[0][1][0][2], la.out[0],
+        rr.pair[1].mid1, panel.go[1][1][0][2], panel.go[0][0][1][3], rr.passed[0][0], ra.outer[0][1].mid0,
+        panel.go[1][0][0][2], ra.outer[1][1].mid0, rr.passed[0][1], panel.go[1][0][1][2], panel.go[0][1][1][3],
+        la.ring[1].start, panel.go[0][0][0][3], rr.passed[0][2], ra.outer[1][0].mid0, ra.outer[1][0].mid1,
+        panel.go[1][1][0][3], ra.outer[0][0].mid0, ra.outer[0][1].mid1, panel.go[0][1][0][3], la.ring[0].mid0,
+        ra.outer[1][1].mid1, panel.go[1][1][1][3], panel.go[1][0][0][3], rr.pair[1].end, ra.take_own, la.ring[0].mid1,
+        panel.go[1][0][1][3], ra.copy_own, rr.passed[0][3], ra.outer[0][0].mid1, la.outer[1][1].start,
+        la.outer[0][1].start, ra.outer[1][0].end, la.pair[1].start, left_r, rr.finish, ra.outer[0][1].end, panel.finish,
+        make_y, ra.outer[1][1].end, ra.outer[0][0].end, ya.ring[0].start, ya.ring[1].start, ya.out[0], ra.finish[0],
+        term_r[0][0], term_r[1][0], zr.step[0][0][0][0], ra.finish[1], term_r[1][1], zr.step[0][1][1][1],
+        zr.step[1][1][0][0], term_r[3][1], zr.step[0][1][1][0], term_r[0][1], zr.step[1][0][1][0], la.outer[0][0].start,
+        la.outer[1][0].start, zr.step[0][0][0][1], ya.out[1], la.outer[1][1].mid0, zr.step[1][0][1][1],
+        la.outer[1][1].mid1, term_r[2][1], la.passed[0][2], la.ring[0].end, la.ring[1].mid0, la.passed[0][0],
+        term_r[3][0], zr.step[0][1][0][0], la.outer[0][1].mid1, ya.ring[1].mid1, zr.step[1][1][1][0], la.copy_own,
+        la.pair[1].mid1, ya.ring[1].mid0, zr.step[1][1][1][1], ya.ring[0].mid1, zr.step[0][1][0][1], la.ring[1].mid1,
+        zr.step[1][1][0][1], ya.ring[0].mid0, zr.step[0][2][1][0], la.outer[0][1].mid0, ya.outer[0][1].start,
+        la.outer[0][0].mid0, zr.step[0][2][1][1], la.pair[1].mid0, la.push_own, term_r[2][0], la.outer[0][0].mid1,
+        zr.step[1][2][0][0], la.outer[1][0].mid0, zr.step[1][2][1][1], zr.step[0][2][0][1], zr.step[0][2][0][0],
+        la.passed[0][3], zr.step[1][2][1][0], ya.outer[0][0].start, ya.outer[1][1].start, ya.passed[1][0],
+        zr.step[1][2][0][1], ya.outer[1][0].start, ya.ring[0].end, ya.outer[0][1].mid1, zr.step[0][3][1][1],
+        zr.step[1][3][1][1], ya.outer[0][1].mid0, ya.push_own, la.outer[1][0].mid1, la.outer[0][0].end,
+        ya.outer[0][0].mid1, zr.step[0][3][1][0], la.outer[1][1].end, la.passed[0][1], la.take_own, zr.step[1][3][0][0],
+        la.outer[0][1].end, zr.step[0][3][0][1], zr.step[1][3][1][0], la.finish[0], ya.outer[0][0].mid0, la.ring[1].end,
+        left_l, zr.step[0][3][0][0], ya.outer[1][1].mid0, ya.outer[1][1].mid1, ya.passed[0][2], ya.passed[0][1],
+        term_l[1][0], ya.copy_own, zr.step[1][3][0][1], la.pair[1].end, ya.ring[1].end, ya.passed[1][1], term_l[0][0],
+        ya.outer[1][0].mid1, ya.passed[0][0], la.finish[1], ya.outer[1][0].mid0, ya.passed[0][3], ya.take_own,
+        ya.outer[0][0].end, ya.outer[0][1].end, la.outer[1][0].end, ya.finish[0], left_y, term_y[1][0], term_y[0][0],
+        zc.step[1][1][0][0], zr.last[1], zr.last[0], zc.step[0][0][0][1], zc.step[0][0][0][0], cc.own,
+        zc.step[1][1][0][1], ya.passed[1][2], term_l[1][1], cc.ring[0].start, cc.ring[1].start, ya.outer[1][1].end,
+        term_l[0][1], ya.outer[1][0].end, ya.passed[1][3], ya.finish[1], term_y[1][1], zc.step[0][1][1][0],
+        term_y[0][1], zc.step[1][0][1][1], zc.step[1][0][1][0], term_l[3][1], term_l[2][0], term_l[2][1], term_y[2][0],
+        zc.step[0][1][0][1], zc.step[0][1][1][1], term_y[2][1], cc.pair[1].start, zc.step[0][1][0][0],
+        zc.step[1][2][0][1], zc.step[1][1][1][1], cc.ring[0].mid1, cc.ring[0].mid0, zc.step[1][1][1][0],
+        zc.step[0][2][1][0], zc.step[0][2][0][1], zc.step[1][2][1][1], zc.step[0][2][0][0], zc.step[1][2][0][0],
+        cc.pair[1].mid0, term_y[3][1], cc.ring[1].mid0, cc.pair[1].mid1, zc.step[1][2][1][0], term_l[3][0],
+        cc.ring[1].mid1, zc.step[0][2][1][1], cc.ring[0].end, term_y[3][0], cc.passed[0][1], zc.step[0][3][1][0],
+        zc.step[1][3][0][1], zc.step[0][3][0][1], zc.step[1][3][0][0], cc.pair[1].end, zc.step[0][3][0][0],
+        zc.step[1][3][1][0], cc.ring[1].end, cc.passed[0][3], zc.step[0][3][1][1], cc.passed[0][0], zc.step[1][3][1][1],
+        cc.passed[0][2], cc.finish, make_cross, zc.last[0], zc.last[1],
     )
     sends.drain()
 
@@ -536,7 +536,7 @@
             pltpu.VMEM((Z,) + half, F32),
             pltpu.VMEM((2, 4) + half, F32),
             pltpu.VMEM((2, 4) + half, F32),
-            dma((24,)),
+            dma((40,)),
             *line,
             *line,
             dma((2, 2, 4)), dma((2, 2)), dma((2,)), dma((1,)),

time: 93.8 us -> 93.3 us (level)
  no operation moved by 1% of the time
where the time goes in v5:
time: 93.3 us; the launch traced here: 93.1 us
  Pallas kernels  92.5 us (99%)
    pallas_call x1, Pallas kernels, shards(): parts = call(structure, root_inv, child_inv, child_panel)  90.5 us
    pallas_call x1, Pallas kernels, shards(): pl.pallas_call(finish, grid=(GRID,), out_shape=(out, out, out), in_specs=...  2 us

profile of v5, /device:TPU:1, one launch (start us, length us, event | category | flops | bytes accessed | tf_op | source)
XLA Modules:
  0.0 93.1 jit_solution(2896955633746546545)
XLA Ops:
  0.6 90.5 %shard_map.67 = (f32[256,256]{1,0:T(8,128)}, f32[256,256]{1,0:T(8,128)}, f32[256,256]{1,0:T(8,128)}) custom-call(s32[16]{0:T(128)} %st.1, f32[256,256]{1,0:T(8,128)} %r.1, f32[256,256]{1,0:T(8,128)} %l.1, f32[128,256]{1,0:T(8,128)} %p.1), custom_call_target="tpu_custom_call" | custom-call | tf_op jit(solution)/shard_map/pallas_call | solution.py:552
  91.1 2.0 %shard_map.68 = (f32[256,256]{1,0:T(8,128)}, f32[256,256]{1,0:T(8,128)}, f32[256,256]{1,0:T(8,128)}) custom-call(f32[256,256]{1,0:T(8,128)} %get-tuple-element.6.a, f32[256,256]{1,0:T(8,128)} %get-tuple-element.7.b, f32[256,256]{1,0:T(8,128)} %get-tuple-element.8.c), custom_call_target="tpu_custom_call" | custom-call | tf_op jit(solution)/shard_map/pallas_call | solution.py:553

commit v6 on v5

--- a/solution.py
+++ b/solution.py
@@ -129,13 +129,12 @@
         at = self.places[1 + side]
         arrived(self.ref(at), self.sems.at[side])
         ref = self.half(at, side)
-        self.sends.go(ref, ref, self.sems.at[2 + side], (self.plus, self.minus)[side], self.kind_half, self.when)
+        self.sends.go(ref, ref, self.sems.at[2], (self.plus, self.minus)[side], self.kind_half, self.when)
         self.got(at, 1 + side)
 
     def last(self):
         at = self.places[3]
-        arrived(self.half(at, 0), self.sems.at[2])
-        arrived(self.half(at, 1), self.sems.at[3])
+        arrived(self.ref(at), self.sems.at[2])
         self.got(at, 3)
 
 
@@ -358,7 +357,7 @@
                                 arrived(got, sems.at[side, n - 1, c, q])
                                 t[pl.ds(d, 1), c, run] += got[...].reshape(1, rows, H)
                             sends.go(
-                                t.at[d, c, run], slots.at[side, n, c, run], sems.at[side, n, c, q],
+                                t.at[d, c, run], slots.at[side, n, c, run], sems.at[side, n, c, q if n < 3 else 0],
                                 zp if side == 0 else zm, slots.at[0, 0, 0, pl.ds(0, rows)],
                             )
 
@@ -366,8 +365,7 @@
 
             def done(c=c):
                 for side in range(2):
-                    for q in range(PIECES):
-                        arrived(slots.at[side, 3, c, pl.ds(rows * q, rows)], sems.at[side, 3, c, q])
+                    arrived(slots.at[side, 3, c], sems.at[side, 3, c, 0])
                 last(c, (t[pl.ds(z, 1), c].reshape(N, H) + slots[0, 3, c] + slots[1, 3, c]).T)
 
             g.last.append(Task(done))

time: 93.3 us -> 93.3 us (level)
  no operation moved by 1% of the time
where the time goes in v6:
time: 93.3 us; the launch traced here: 93.1 us
  Pallas kernels  92.5 us (99%)
    pallas_call x1, Pallas kernels, shards(): parts = call(structure, root_inv, child_inv, child_panel)  90.5 us
    pallas_call x1, Pallas kernels, shards(): pl.pallas_call(finish, grid=(GRID,), out_shape=(out, out, out), in_specs=...  2 us

profile of v6, /device:TPU:1, one launch (start us, length us, event | category | flops | bytes accessed | tf_op | source)
XLA Modules:
  0.0 93.1 jit_solution(4175848983672321550)
XLA Ops:
  0.6 90.5 %shard_map.67 = (f32[256,256]{1,0:T(8,128)}, f32[256,256]{1,0:T(8,128)}, f32[256,256]{1,0:T(8,128)}) custom-call(s32[16]{0:T(128)} %st.1, f32[256,256]{1,0:T(8,128)} %r.1, f32[256,256]{1,0:T(8,128)} %l.1, f32[128,256]{1,0:T(8,128)} %p.1), custom_call_target="tpu_custom_call" | custom-call | tf_op jit(solution)/shard_map/pallas_call | solution.py:550
  91.1 2.0 %shard_map.68 = (f32[256,256]{1,0:T(8,128)}, f32[256,256]{1,0:T(8,128)}, f32[256,256]{1,0:T(8,128)}) custom-call(f32[256,256]{1,0:T(8,128)} %get-tuple-element.6.a, f32[256,256]{1,0:T(8,128)} %get-tuple-element.7.b, f32[256,256]{1,0:T(8,128)} %get-tuple-element.8.c), custom_call_target="tpu_custom_call" | custom-call | tf_op jit(solution)/shard_map/pallas_call | solution.py:551
